TPU v7x, 32 devices: a whole 2x2x4 slice. The times are simulated.
32 devices in a mesh: batch: 2 (over core), seq: 16 (over z, y, x).
Axes of the slice: x: 2, y: 2, z: 4, core: 2. Of those that a mesh axis runs over, the one named last changes fastest.
Arguments:
- tokens: bfloat16 [4, 2048, 768], P('batch', 'seq'), may hold values from -6 to 6
- doc_lengths: int32 [4, 8], P('batch'), may hold values from 0 to 2048, as said below
- query_weight: bfloat16 [768, 768], P(('batch', 'seq')), may hold values from -0.21875 to 0.21875
- query_bias: bfloat16 [768], P(('batch', 'seq')), may hold values from -3 to 3
- key_weight: bfloat16 [768, 768], P(('batch', 'seq')), may hold values from -0.21875 to 0.21875
- value_weight: bfloat16 [768, 768], P(('batch', 'seq')), may hold values from -0.21875 to 0.21875
- value_bias: bfloat16 [768], P(('batch', 'seq')), may hold values from -0.59765625 to 0.59765625
- output_weight: bfloat16 [768, 768], P(('batch', 'seq')), may hold values from -1.75 to 1.75
- output_bias: bfloat16 [768], P(('batch', 'seq')), may hold values from -2 to 2
- attn_gain: bfloat16 [768], P(('batch', 'seq')), may hold values from 0.25 to 1.75
- attn_shift: bfloat16 [768], P(('batch', 'seq')), may hold values from -2 to 2
- up_weight: bfloat16 [768, 3072], P(('batch', 'seq')), may hold values from -0.21875 to 0.21875
- up_bias: bfloat16 [3072], P(('batch', 'seq')), may hold values from -2 to 2
- down_weight: bfloat16 [3072, 768], P(('batch', 'seq')), may hold values from -0.109375 to 0.109375
- down_bias: bfloat16 [768], P(('batch', 'seq')), may hold values from -2 to 2
- ffn_gain: bfloat16 [768], P(('batch', 'seq')), may hold values from 0.25 to 1.75
- ffn_shift: bfloat16 [768], P(('batch', 'seq')), may hold values from -2 to 2
- cotangent: bfloat16 [4, 2048, 768], P('batch', 'seq'), may hold values from -6 to 6
Outputs:
- mixed: bfloat16 [4, 2048, 768], P('batch', 'seq')
- grad_tokens: float32 [4, 2048, 768], P('batch', 'seq')
- grad_query_weight: float32 [768, 768], P(('batch', 'seq'))
- grad_query_bias: float32 [768], P(('batch', 'seq'))
- grad_key_weight: float32 [768, 768], P(('batch', 'seq'))
- grad_value_weight: float32 [768, 768], P(('batch', 'seq'))
- grad_value_bias: float32 [768], P(('batch', 'seq'))
- grad_output_weight: float32 [768, 768], P(('batch', 'seq'))
- grad_output_bias: float32 [768], P(('batch', 'seq'))
- grad_attn_gain: float32 [768], P(('batch', 'seq'))
- grad_attn_shift: float32 [768], P(('batch', 'seq'))
- grad_up_weight: float32 [768, 3072], P(('batch', 'seq'))
- grad_up_bias: float32 [3072], P(('batch', 'seq'))
- grad_down_weight: float32 [3072, 768], P(('batch', 'seq'))
- grad_down_bias: float32 [768], P(('batch', 'seq'))
- grad_ffn_gain: float32 [768], P(('batch', 'seq'))
- grad_ffn_shift: float32 [768], P(('batch', 'seq'))
Inputs may be any that keep to these rules, and one draw needn't show every extreme that they name: Each row of doc_lengths sums to 2048; a document may be empty.
All inputs are finite; a program needn't handle non-finite values.
Results may differ from a plain program's by a relative error of at most 0.014.
Values may be sent and summed in bfloat16 or wider, within the bound.
No kernel may reach another device: no remote copies, remote signals or barrier semaphores. Data moves between devices by JAX's collectives and lax.ppermute only.
A program may use at most 192 MiB of HBM per device.

v0:
```python
import jax
import jax.numpy as jnp
from jax import lax
from jax.experimental import pallas as pl
from jax.experimental.pallas import tpu as pltpu
from jax.sharding import PartitionSpec as P

HEADS = 12
HEAD_DIM = 64


SCALE = 0.125
NEG = -1e30
EPS = 1e-12


def norm_apply(hidden, gain_vec, shift_vec):
    center = jnp.mean(hidden, axis=-1, keepdims=True)
    centered = hidden - center
    spread = jnp.mean(centered * centered, axis=-1, keepdims=True)
    return centered * lax.rsqrt(spread + EPS) * gain_vec + shift_vec


def gelu_exact(inputs):
    return jax.nn.gelu(inputs, approximate=False)


def segment_ids(doc_lengths, positions):
    doc_ends = jnp.cumsum(doc_lengths, axis=-1)
    return jnp.sum((positions[None, :, None] >= doc_ends[:, None, :]).astype(jnp.int32), axis=-1)


def matmul_plain(left_op, right_op):
    return jnp.dot(left_op, right_op, preferred_element_type=jnp.float32)


def matmul_right_t(left_op, right_op):
    return lax.dot_general(
        left_op, right_op, (((1,), (1,)), ((), ())), preferred_element_type=jnp.float32
    )


def matmul_left_t(left_op, right_op):
    return lax.dot_general(
        left_op, right_op, (((0,), (0,)), ((), ())), preferred_element_type=jnp.float32
    )


def column_sums(matrix):
    return jnp.sum(matrix.astype(jnp.float32), axis=0)


def head_block(matrix, head_pair):
    pair_width = 2 * HEAD_DIM
    column_block = matrix[..., head_pair * pair_width : (head_pair + 1) * pair_width]
    return column_block.reshape(column_block.shape[:-1] + (2, HEAD_DIM))


def merge_heads(blocks):
    return jnp.concatenate(
        [block_item.reshape(block_item.shape[:2] + (2 * HEAD_DIM,)) for block_item in blocks],
        axis=-1,
    )


def stat_pair(stats, head_pair):
    return stats[:, 2 * head_pair : 2 * head_pair + 2][..., None]


def pair_scores(query_pair, key_pair, same_doc):
    raw_scores = jnp.einsum(
        "sqhd,skhd->shqk", query_pair, key_pair, preferred_element_type=jnp.float32
    )
    return jnp.where(same_doc[:, None], SCALE * raw_scores, NEG)


def attend_forward(queries, key_all, value_all, same_doc):
    outputs, log_sums = ([], [])
    for head_pair in range(HEADS // 2):
        scores = pair_scores(
            head_block(queries, head_pair), head_block(key_all, head_pair), same_doc
        )
        top_score = jnp.max(scores, axis=-1, keepdims=True)
        exponent = jnp.exp(scores - top_score)
        totals = jnp.sum(exponent, axis=-1, keepdims=True)
        probs_low = (exponent / totals).astype(jnp.bfloat16)
        context = jnp.einsum(
            "shqk,skhd->sqhd",
            probs_low,
            head_block(value_all, head_pair),
            preferred_element_type=jnp.float32,
        )
        outputs.append(context)
        log_sums.append((top_score + jnp.log(totals))[..., 0])
    return (merge_heads(outputs), jnp.concatenate(log_sums, axis=1))


def attend_backward(queries, key_all, value_all, same_doc, log_sums, grad_context):
    query_grads, key_grads, value_grads, row_dots = ([], [], [], [])
    for head_pair in range(HEADS // 2):
        query_pair = head_block(queries, head_pair)
        key_pair = head_block(key_all, head_pair)
        grad_pair = head_block(grad_context, head_pair)
        probs = jnp.exp(
            pair_scores(query_pair, key_pair, same_doc) - stat_pair(log_sums, head_pair)
        )
        grad_probs = jnp.einsum(
            "sqhd,skhd->shqk",
            grad_pair,
            head_block(value_all, head_pair),
            preferred_element_type=jnp.float32,
        )
        row_dot = jnp.sum(probs * grad_probs, axis=-1, keepdims=True)
        row_dots.append(row_dot[..., 0])
        grad_scores = (probs * (grad_probs - row_dot)).astype(jnp.bfloat16) * jnp.bfloat16(SCALE)
        query_grads.append(
            jnp.einsum("shqk,skhd->sqhd", grad_scores, key_pair, preferred_element_type=jnp.float32)
        )
    return (merge_heads(query_grads), jnp.concatenate(row_dots, axis=1), None, None)


def key_side_local(query_all, grad_ctx_all, lse_all, rowdot_all, keys_own, values_own, same_doc_t):
    key_grads, value_grads = ([], [])
    for head_pair in range(HEADS // 2):
        query_pair = head_block(query_all, head_pair)
        grad_pair = head_block(grad_ctx_all, head_pair)
        probs = jnp.exp(
            pair_scores(query_pair, head_block(keys_own, head_pair), same_doc_t)
            - stat_pair(lse_all, head_pair)
        )
        grad_probs = jnp.einsum(
            "sqhd,skhd->shqk",
            grad_pair,
            head_block(values_own, head_pair),
            preferred_element_type=jnp.float32,
        )
        grad_scores = (probs * (grad_probs - stat_pair(rowdot_all, head_pair))).astype(
            jnp.bfloat16
        ) * jnp.bfloat16(SCALE)
        key_grads.append(
            jnp.einsum(
                "shqk,sqhd->skhd", grad_scores, query_pair, preferred_element_type=jnp.float32
            )
        )
        value_grads.append(
            jnp.einsum(
                "shqk,sqhd->skhd",
                probs.astype(jnp.bfloat16),
                grad_pair,
                preferred_element_type=jnp.float32,
            )
        )
    return (merge_heads(key_grads), merge_heads(value_grads))


def shards_general(
    tokens,
    doc_lengths,
    query_weight,
    query_bias,
    key_weight,
    value_weight,
    value_bias,
    output_weight,
    output_bias,
    attn_gain,
    attn_shift,
    up_weight,
    up_bias,
    down_weight,
    down_bias,
    ffn_gain,
    ffn_shift,
    cotangent,
):
    gathered = (
        lax.all_gather(query_weight, ("batch", "seq"), axis=0, tiled=True),
        lax.all_gather(query_bias, ("batch", "seq"), axis=0, tiled=True),
        lax.all_gather(key_weight, ("batch", "seq"), axis=0, tiled=True),
        lax.all_gather(value_weight, ("batch", "seq"), axis=0, tiled=True),
        lax.all_gather(value_bias, ("batch", "seq"), axis=0, tiled=True),
        lax.all_gather(output_weight, ("batch", "seq"), axis=0, tiled=True),
        lax.all_gather(output_bias, ("batch", "seq"), axis=0, tiled=True),
        lax.all_gather(attn_gain, ("batch", "seq"), axis=0, tiled=True),
        lax.all_gather(attn_shift, ("batch", "seq"), axis=0, tiled=True),
        lax.all_gather(up_weight, ("batch", "seq"), axis=0, tiled=True),
        lax.all_gather(up_bias, ("batch", "seq"), axis=0, tiled=True),
        lax.all_gather(down_weight, ("batch", "seq"), axis=0, tiled=True),
        lax.all_gather(down_bias, ("batch", "seq"), axis=0, tiled=True),
        lax.all_gather(ffn_gain, ("batch", "seq"), axis=0, tiled=True),
        lax.all_gather(ffn_shift, ("batch", "seq"), axis=0, tiled=True),
    )
    (
        query_full,
        qbias_full,
        key_full,
        value_full,
        vbias_full,
        output_full,
        obias_full,
        again_full,
        ashift_full,
        up_full,
        ubias_full,
        down_full,
        dbias_full,
        fgain_full,
        fshift_full,
    ) = gathered
    seq_groups, stretch_len, width = tokens.shape
    row_count = seq_groups * stretch_len
    token_rows = tokens.reshape(row_count, width)
    positions = lax.axis_index("seq") * stretch_len + jnp.arange(stretch_len, dtype=jnp.int32)
    total_len = stretch_len * lax.axis_size("seq")
    query_seg = segment_ids(doc_lengths, positions)
    key_seg = segment_ids(doc_lengths, jnp.arange(total_len, dtype=jnp.int32))
    same_doc = query_seg[:, :, None] == key_seg[:, None, :]
    queries = (
        (matmul_plain(token_rows, query_full) + qbias_full)
        .astype(jnp.bfloat16)
        .reshape(tokens.shape)
    )
    keys_local = matmul_plain(token_rows, key_full).astype(jnp.bfloat16).reshape(tokens.shape)
    values_local = (
        (matmul_plain(token_rows, value_full) + vbias_full)
        .astype(jnp.bfloat16)
        .reshape(tokens.shape)
    )
    key_all, value_all = (
        lax.all_gather(keys_local, "seq", axis=1, tiled=True),
        lax.all_gather(values_local, "seq", axis=1, tiled=True),
    )
    context, log_sums = attend_forward(queries, key_all, value_all, same_doc)
    context_low = context.reshape(row_count, width).astype(jnp.bfloat16)
    res_one = token_rows.astype(jnp.float32) + matmul_plain(context_low, output_full) + obias_full
    normed, pull_one = jax.vjp(
        norm_apply, res_one, again_full.astype(jnp.float32), ashift_full.astype(jnp.float32)
    )
    normed_low = normed.astype(jnp.bfloat16)
    up_pre = matmul_plain(normed_low, up_full) + ubias_full
    activated, pull_gelu = jax.vjp(gelu_exact, up_pre)
    act_low = activated.astype(jnp.bfloat16)
    res_two = normed + matmul_plain(act_low, down_full) + dbias_full
    output_rows, pull_two = jax.vjp(
        norm_apply, res_two, fgain_full.astype(jnp.float32), fshift_full.astype(jnp.float32)
    )
    mixed = output_rows.astype(jnp.bfloat16).reshape(tokens.shape)
    regathered = (
        lax.all_gather(query_weight, ("batch", "seq"), axis=0, tiled=True),
        lax.all_gather(query_bias, ("batch", "seq"), axis=0, tiled=True),
        lax.all_gather(key_weight, ("batch", "seq"), axis=0, tiled=True),
        lax.all_gather(value_weight, ("batch", "seq"), axis=0, tiled=True),
        lax.all_gather(value_bias, ("batch", "seq"), axis=0, tiled=True),
        lax.all_gather(output_weight, ("batch", "seq"), axis=0, tiled=True),
        lax.all_gather(output_bias, ("batch", "seq"), axis=0, tiled=True),
        lax.all_gather(attn_gain, ("batch", "seq"), axis=0, tiled=True),
        lax.all_gather(attn_shift, ("batch", "seq"), axis=0, tiled=True),
        lax.all_gather(up_weight, ("batch", "seq"), axis=0, tiled=True),
        lax.all_gather(up_bias, ("batch", "seq"), axis=0, tiled=True),
        lax.all_gather(down_weight, ("batch", "seq"), axis=0, tiled=True),
        lax.all_gather(down_bias, ("batch", "seq"), axis=0, tiled=True),
        lax.all_gather(ffn_gain, ("batch", "seq"), axis=0, tiled=True),
        lax.all_gather(ffn_shift, ("batch", "seq"), axis=0, tiled=True),
    )
    query_back = regathered[0]
    key_back = regathered[2]
    value_back = regathered[3]
    output_back = regathered[5]
    up_back = regathered[9]
    down_back = regathered[11]
    grad_out = cotangent.astype(jnp.float32).reshape(row_count, width)
    grad_res_two, grad_ffn_gain, grad_ffn_shift = pull_two(grad_out)
    grad_down_low = grad_res_two.astype(jnp.bfloat16)
    grad_down_weight = matmul_left_t(act_low, grad_down_low)
    grad_down_bias = column_sums(grad_down_low)
    (grad_up_pre,) = pull_gelu(matmul_right_t(grad_down_low, down_back))
    grad_up_low = grad_up_pre.astype(jnp.bfloat16)
    grad_up_weight = matmul_left_t(normed_low, grad_up_low)
    grad_up_bias = column_sums(grad_up_low)
    grad_normed = grad_res_two + matmul_right_t(grad_up_low, up_back)
    grad_res_one, grad_attn_gain, grad_attn_shift = pull_one(grad_normed)
    grad_branch_low = grad_res_one.astype(jnp.bfloat16)
    grad_output_weight = matmul_left_t(context_low, grad_branch_low)
    grad_output_bias = column_sums(grad_branch_low)
    grad_context = (
        matmul_right_t(grad_branch_low, output_back).astype(jnp.bfloat16).reshape(tokens.shape)
    )
    key_again, value_again = (
        lax.all_gather(keys_local, "seq", axis=1, tiled=True),
        lax.all_gather(values_local, "seq", axis=1, tiled=True),
    )
    grad_query, row_dots, unused_key, unused_value = attend_backward(
        queries, key_again, value_again, same_doc, log_sums, grad_context
    )
    query_all, grad_ctx_all = (
        lax.all_gather(queries, "seq", axis=1, tiled=True),
        lax.all_gather(grad_context, "seq", axis=1, tiled=True),
    )
    lse_all, rowdot_all = (
        lax.all_gather(log_sums, "seq", axis=2, tiled=True),
        lax.all_gather(row_dots, "seq", axis=2, tiled=True),
    )
    same_doc_t = key_seg[:, :, None] == query_seg[:, None, :]
    grad_key, grad_value = key_side_local(
        query_all, grad_ctx_all, lse_all, rowdot_all, keys_local, values_local, same_doc_t
    )
    grad_query_low = grad_query.reshape(row_count, width).astype(jnp.bfloat16)
    grad_key_low = grad_key.reshape(row_count, width).astype(jnp.bfloat16)
    grad_value_low = grad_value.reshape(row_count, width).astype(jnp.bfloat16)
    grad_query_weight = matmul_left_t(token_rows, grad_query_low)
    grad_query_bias = column_sums(grad_query_low)
    grad_key_weight = matmul_left_t(token_rows, grad_key_low)
    grad_value_weight = matmul_left_t(token_rows, grad_value_low)
    grad_value_bias = column_sums(grad_value_low)
    grad_tokens = (
        grad_res_one
        + matmul_right_t(grad_query_low, query_back)
        + matmul_right_t(grad_key_low, key_back)
        + matmul_right_t(grad_value_low, value_back)
    )
    summed = (
        lax.psum_scatter(grad_query_weight, ("batch", "seq"), scatter_dimension=0, tiled=True),
        lax.psum_scatter(grad_query_bias, ("batch", "seq"), scatter_dimension=0, tiled=True),
        lax.psum_scatter(grad_key_weight, ("batch", "seq"), scatter_dimension=0, tiled=True),
        lax.psum_scatter(grad_value_weight, ("batch", "seq"), scatter_dimension=0, tiled=True),
        lax.psum_scatter(grad_value_bias, ("batch", "seq"), scatter_dimension=0, tiled=True),
        lax.psum_scatter(grad_output_weight, ("batch", "seq"), scatter_dimension=0, tiled=True),
        lax.psum_scatter(grad_output_bias, ("batch", "seq"), scatter_dimension=0, tiled=True),
        lax.psum_scatter(grad_attn_gain, ("batch", "seq"), scatter_dimension=0, tiled=True),
        lax.psum_scatter(grad_attn_shift, ("batch", "seq"), scatter_dimension=0, tiled=True),
        lax.psum_scatter(grad_up_weight, ("batch", "seq"), scatter_dimension=0, tiled=True),
        lax.psum_scatter(grad_up_bias, ("batch", "seq"), scatter_dimension=0, tiled=True),
        lax.psum_scatter(grad_down_weight, ("batch", "seq"), scatter_dimension=0, tiled=True),
        lax.psum_scatter(grad_down_bias, ("batch", "seq"), scatter_dimension=0, tiled=True),
        lax.psum_scatter(grad_ffn_gain, ("batch", "seq"), scatter_dimension=0, tiled=True),
        lax.psum_scatter(grad_ffn_shift, ("batch", "seq"), scatter_dimension=0, tiled=True),
    )
    return (
        mixed,
        grad_tokens.reshape(tokens.shape),
        summed[0],
        summed[1],
        summed[2],
        summed[3],
        summed[4],
        summed[5],
        summed[6],
        summed[7],
        summed[8],
        summed[9],
        summed[10],
        summed[11],
        summed[12],
        summed[13],
        summed[14],
    )


LOG2E = 1.4426950408889634
GROUP_HEADS = 3
GROUP_COLS = GROUP_HEADS * HEAD_DIM
PACK = 640
VECS = 12
SIDE = 16
KEY_CHUNK = 512


def dot_nt(left_op, right_op):
    return lax.dot_general(
        left_op, right_op, (((1,), (1,)), ((), ())), preferred_element_type=jnp.float32
    )


def dot_nn(left_op, right_op):
    return lax.dot_general(
        left_op, right_op, (((1,), (0,)), ((), ())), preferred_element_type=jnp.float32
    )


def attend_kernel(
    query_ref, own_ref, other_ref, seg_key_ref, seg_query_ref, ctx_ref, lse_ref, value_t
):
    half = own_ref.shape[0]
    rows = query_ref.shape[0]

    @pl.when(pl.program_id(0) == 0)
    def _():
        value_t[:, :half] = own_ref[:, GROUP_COLS : 2 * GROUP_COLS].T
        value_t[:, half:] = other_ref[:, GROUP_COLS : 2 * GROUP_COLS].T

    seg_query = seg_query_ref[...]
    chunks = [
        (ref, start) for ref in (own_ref, other_ref) for start in range(0, half, KEY_CHUNK)
    ]
    for head in range(GROUP_HEADS):
        cols = slice(head * HEAD_DIM, (head + 1) * HEAD_DIM)
        query = query_ref[:, cols]
        scores = []
        top = None
        for number, (ref, start) in enumerate(chunks):
            raw = dot_nt(ref[start : start + KEY_CHUNK, cols], query)
            seg_key = seg_key_ref[number * KEY_CHUNK : (number + 1) * KEY_CHUNK, :]
            seg_key = jnp.concatenate([seg_key] * (rows // 128), axis=1)
            masked = jnp.where(seg_key == seg_query, raw * (SCALE * LOG2E), NEG)
            scores.append(masked)
            peak = jnp.max(masked, axis=0, keepdims=True)
            top = peak if top is None else jnp.maximum(top, peak)
        total = None
        context_t = None
        for number in range(len(chunks)):
            weight = jnp.exp2(scores[number] - top)
            part = jnp.sum(weight, axis=0, keepdims=True)
            piece = dot_nn(
                value_t[cols, number * KEY_CHUNK : (number + 1) * KEY_CHUNK],
                weight.astype(jnp.bfloat16),
            )
            total = part if total is None else total + part
            context_t = piece if context_t is None else context_t + piece
        ctx_ref[:, cols] = (context_t / total).T
        lse_ref[head : head + 1, :] = top + jnp.log2(total)


def attend(query, own, other, seg_key, seg_query):
    rows = query.shape[0]
    half = own.shape[0]
    block = rows // 4
    return pl.pallas_call(
        attend_kernel,
        grid=(4,),
        in_specs=[
            pl.BlockSpec((block, GROUP_COLS), lambda i: (i, 0)),
            pl.BlockSpec((half, 2 * GROUP_COLS), lambda i: (0, 0)),
            pl.BlockSpec((half, 2 * GROUP_COLS), lambda i: (0, 0)),
            pl.BlockSpec((2 * half, 128), lambda i: (0, 0)),
            pl.BlockSpec((1, block), lambda i: (0, i)),
        ],
        out_specs=[
            pl.BlockSpec((block, GROUP_COLS), lambda i: (i, 0)),
            pl.BlockSpec((8, block), lambda i: (0, i)),
        ],
        out_shape=[
            jax.ShapeDtypeStruct((rows, GROUP_COLS), jnp.float32),
            jax.ShapeDtypeStruct((8, rows), jnp.float32),
        ],
        scratch_shapes=[pltpu.VMEM((GROUP_COLS, 2 * half), jnp.bfloat16)],
        compiler_params=pltpu.CompilerParams(vmem_limit_bytes=48 * 1024 * 1024),
        cost_estimate=pl.CostEstimate(
            flops=16 * rows * half * GROUP_COLS,
            bytes_accessed=4 * 1024 * 1024,
            transcendentals=2 * GROUP_HEADS * rows * half,
        ),
        name="attend",
    )(query, own, other, seg_key, seg_query)


def attend_back_kernel(
    query_ref,
    grad_ref,
    ctx_ref,
    lse_ref,
    own_ref,
    other_ref,
    seg_key_ref,
    seg_query_ref,
    gquery_ref,
    gown_ref,
    gother_ref,
    key_t,
):
    half = own_ref.shape[0]
    rows = query_ref.shape[0]
    first = pl.program_id(0) == 0

    @pl.when(first)
    def _():
        key_t[:, :half] = own_ref[:, :GROUP_COLS].T
        key_t[:, half:] = other_ref[:, :GROUP_COLS].T
        gown_ref[...] = jnp.zeros_like(gown_ref)
        gother_ref[...] = jnp.zeros_like(gother_ref)

    seg_query = seg_query_ref[...]
    chunks = [
        (ref, gref, start)
        for ref, gref in ((own_ref, gown_ref), (other_ref, gother_ref))
        for start in range(0, half, KEY_CHUNK)
    ]
    for head in range(GROUP_HEADS):
        cols = slice(head * HEAD_DIM, (head + 1) * HEAD_DIM)
        vcols = slice(GROUP_COLS + head * HEAD_DIM, GROUP_COLS + (head + 1) * HEAD_DIM)
        query = query_ref[:, cols]
        grad = grad_ref[:, cols]
        lse = lse_ref[head : head + 1, :]
        dots = (grad.astype(jnp.float32) * ctx_ref[:, cols]).T
        row_dot = jnp.sum(dots, axis=0, keepdims=True)
        gquery_t = None
        for number, (ref, gref, start) in enumerate(chunks):
            spot = slice(start, start + KEY_CHUNK)
            raw = dot_nt(ref[spot, cols], query)
            seg_key = seg_key_ref[number * KEY_CHUNK : (number + 1) * KEY_CHUNK, :]
            seg_key = jnp.concatenate([seg_key] * (rows // 128), axis=1)
            masked = jnp.where(seg_key == seg_query, raw * (SCALE * LOG2E), NEG)
            probs = jnp.exp2(masked - lse)
            gprobs = dot_nt(ref[spot, vcols], grad)
            gscores = (probs * (gprobs - row_dot)).astype(jnp.bfloat16)
            gref[spot, vcols] += dot_nn(probs.astype(jnp.bfloat16), grad)
            gref[spot, cols] += dot_nn(gscores, query)
            piece = dot_nn(key_t[cols, number * KEY_CHUNK : (number + 1) * KEY_CHUNK], gscores)
            gquery_t = piece if gquery_t is None else gquery_t + piece
        gquery_ref[:, cols] = (SCALE * gquery_t).T


def attend_back(query, grad, ctx, lse, own, other, seg_key, seg_query):
    rows = query.shape[0]
    half = own.shape[0]
    block = rows // 4
    return pl.pallas_call(
        attend_back_kernel,
        grid=(4,),
        in_specs=[
            pl.BlockSpec((block, GROUP_COLS), lambda i: (i, 0)),
            pl.BlockSpec((block, GROUP_COLS), lambda i: (i, 0)),
            pl.BlockSpec((block, GROUP_COLS), lambda i: (i, 0)),
            pl.BlockSpec((8, block), lambda i: (0, i)),
            pl.BlockSpec((half, 2 * GROUP_COLS), lambda i: (0, 0)),
            pl.BlockSpec((half, 2 * GROUP_COLS), lambda i: (0, 0)),
            pl.BlockSpec((2 * half, 128), lambda i: (0, 0)),
            pl.BlockSpec((1, block), lambda i: (0, i)),
        ],
        out_specs=[
            pl.BlockSpec((block, GROUP_COLS), lambda i: (i, 0)),
            pl.BlockSpec((half, 2 * GROUP_COLS), lambda i: (0, 0)),
            pl.BlockSpec((half, 2 * GROUP_COLS), lambda i: (0, 0)),
        ],
        out_shape=[
            jax.ShapeDtypeStruct((rows, GROUP_COLS), jnp.float32),
            jax.ShapeDtypeStruct((half, 2 * GROUP_COLS), jnp.float32),
            jax.ShapeDtypeStruct((half, 2 * GROUP_COLS), jnp.float32),
        ],
        scratch_shapes=[pltpu.VMEM((GROUP_COLS, 2 * half), jnp.bfloat16)],
        compiler_params=pltpu.CompilerParams(vmem_limit_bytes=48 * 1024 * 1024),
        cost_estimate=pl.CostEstimate(
            flops=40 * rows * half * GROUP_COLS,
            bytes_accessed=10 * 1024 * 1024,
            transcendentals=2 * GROUP_HEADS * rows * half,
        ),
        name="attend_back",
    )(query, grad, ctx, lse, own, other, seg_key, seg_query)


def prepare_kernel(
    tokens_ref,
    lengths_ref,
    key_ref,
    value_ref,
    query_ref,
    qbias_ref,
    vbias_ref,
    obias_ref,
    again_ref,
    ashift_ref,
    dbias_ref,
    fgain_ref,
    fshift_ref,
    ubias_ref,
    first_ref,
    second_ref,
    *piece_refs,
):
    place = lax.axis_index("seq")
    odd = lax.rem(place // 4, 2) == 1
    quad = lax.rem(place, 4)
    first_ref[...] = jnp.where(odd, tokens_ref[1], tokens_ref[0])
    second_ref[...] = jnp.where(odd, tokens_ref[0], tokens_ref[1])
    own_rows = key_ref.shape[0]
    small = (qbias_ref, vbias_ref, obias_ref, again_ref, ashift_ref, dbias_ref, fgain_ref, fshift_ref)
    rows = [ref[...].astype(jnp.float32) for ref in small]
    wide = ubias_ref[...].astype(jnp.float32)
    rows += [wide[:, n * own_rows : (n + 1) * own_rows] for n in range(VECS - len(small))]
    lengths = lengths_ref[...]
    docs = lengths.shape[1]
    flat = jnp.concatenate(
        [lengths[0:1], lengths[1:2], jnp.zeros((1, own_rows - 2 * docs), jnp.int32)], axis=1
    )
    rows += [(flat >> 6).astype(jnp.float32), (flat & 63).astype(jnp.float32)]
    rows += [jnp.zeros_like(rows[0])] * (SIDE - len(rows))
    side = jnp.concatenate(rows, axis=0).T.astype(jnp.bfloat16)
    cut = 3 * GROUP_COLS
    for flip, piece_ref in enumerate(piece_refs):
        piece_ref[...] = jnp.zeros_like(piece_ref)
        piece_ref[:, cut : cut + SIDE] = side
        target = quad ^ flip
        for number in range(4):

            @pl.when(target == number)
            def _():
                cols = slice(number * GROUP_COLS, (number + 1) * GROUP_COLS)
                for spot, ref in enumerate((key_ref, value_ref, query_ref)):
                    piece_ref[:, spot * GROUP_COLS : (spot + 1) * GROUP_COLS] = ref[:, cols]


def prepare(tokens, lengths, key, value, query, vectors, up_bias):
    own_rows = key.shape[0]
    turn_shape = jax.ShapeDtypeStruct(tokens.shape[1:], jnp.bfloat16)
    piece_shape = jax.ShapeDtypeStruct((own_rows, PACK), jnp.bfloat16)
    return pl.pallas_call(
        prepare_kernel,
        out_shape=[turn_shape] * 2 + [piece_shape] * 4,
        name="prepare",
    )(
        tokens,
        lengths,
        key,
        value,
        query,
        *[item.reshape(1, own_rows) for item in vectors],
        up_bias.reshape(1, up_bias.shape[0]),
    )


def scatter_sum(term, rows, core, layer_z, quad):
    theirs = term(1 - core).astype(jnp.bfloat16)
    total = (term(core) + hop_core(theirs).astype(jnp.float32)).astype(jnp.bfloat16)
    blocks = total.reshape(4, 4, rows, total.shape[-1])

    def block(values, index, axis):
        return lax.dynamic_index_in_dim(values, index, axis=axis, keepdims=False)

    part = block(blocks, quad, 1).astype(jnp.float32)
    for flip in (1, 2, 3):
        part = part + hop_quad(block(blocks, quad ^ flip, 1), flip).astype(jnp.float32)
    blocks = part.astype(jnp.bfloat16)
    part = block(part, layer_z, 0)
    for flip in (1, 2, 3):
        part = part + hop_layer(block(blocks, layer_z ^ flip, 0), flip).astype(jnp.float32)
    return part


def device_table(mapping):
    pairs = []
    for core in range(2):
        for layer_z in range(4):
            for quad in range(4):
                to_core, to_z, to_quad = mapping(core, layer_z, quad)
                pairs.append((core * 16 + layer_z * 4 + quad, to_core * 16 + to_z * 4 + to_quad))
    return pairs


def hop(value, mapping):
    return lax.ppermute(value, ("batch", "seq"), device_table(mapping))


def hop_quad(value, flip):
    return hop(value, lambda core, layer_z, quad: (core, layer_z, quad ^ flip))


def hop_layer(value, flip):
    return hop(value, lambda core, layer_z, quad: (core, layer_z ^ flip, quad))


def hop_core(value):
    return hop(value, lambda core, layer_z, quad: (1 - core, layer_z, quad))


def to_sequence(value, turn):
    return hop(
        value,
        lambda core, layer_z, quad: (layer_z // 2, 2 * core + (layer_z + turn) % 2, quad),
    )


def to_owner(value, turn):
    return hop(
        value,
        lambda core, layer_z, quad: (layer_z // 2, 2 * core + (layer_z - turn) % 2, quad),
    )


def turned(blocks, quad):
    first, second, third, fourth = blocks
    odd = quad % 2 == 1
    high = quad // 2 == 1
    pairs = (
        jnp.where(odd, second, first),
        jnp.where(odd, first, second),
        jnp.where(odd, fourth, third),
        jnp.where(odd, third, fourth),
    )
    return (
        jnp.where(high, pairs[2], pairs[0]),
        jnp.where(high, pairs[3], pairs[1]),
        jnp.where(high, pairs[0], pairs[2]),
        jnp.where(high, pairs[1], pairs[3]),
    )


def pack_grads(main, vecs):
    coarse = vecs.astype(jnp.bfloat16)
    fine = (vecs - coarse.astype(jnp.float32)).astype(jnp.bfloat16)
    filler = jnp.zeros(main.shape[:-1] + (PACK - main.shape[-1] - 2 * VECS,), jnp.bfloat16)
    return jnp.concatenate([main.astype(jnp.bfloat16), coarse, fine, filler], axis=-1)


def unpack_grads(packed):
    wide = packed.astype(jnp.float32)
    cut = 3 * GROUP_COLS
    return (wide[..., :cut], wide[..., cut : cut + VECS] + wide[..., cut + VECS : cut + 2 * VECS])


def shards_heads(
    tokens,
    doc_lengths,
    query_weight,
    query_bias,
    key_weight,
    value_weight,
    value_bias,
    output_weight,
    output_bias,
    attn_gain,
    attn_shift,
    up_weight,
    up_bias,
    down_weight,
    down_bias,
    ffn_gain,
    ffn_shift,
    cotangent,
):
    groups, stretch, width = tokens.shape
    own_rows = query_weight.shape[0]
    hidden = up_weight.shape[1]
    ratio = hidden // width
    devices = width // own_rows
    bulk_rows = own_rows * (1 + 2 * ratio)
    row_count = groups * stretch
    core = lax.axis_index("batch")
    place = lax.axis_index("seq")
    layer_z = place // 4
    quad = place % 4
    parity = layer_z % 2
    flips = (1, 2, 3)

    vectors = (
        query_bias,
        value_bias,
        output_bias,
        attn_gain,
        attn_shift,
        down_bias,
        ffn_gain,
        ffn_shift,
    )
    first_turn, second_turn, *pieces = prepare(
        tokens, doc_lengths, key_weight, value_weight, query_weight, vectors, up_bias
    )

    with jax.named_scope("tokens_out"):
        own_block = jnp.concatenate(
            [to_sequence(first_turn, 0), to_sequence(second_turn, 1)], axis=0
        )
        token_half = jnp.concatenate(
            [own_block] + [hop_quad(own_block, flip) for flip in flips], axis=0
        )

    with jax.named_scope("group_weights"):
        quads = turned([pieces[0]] + [hop_quad(pieces[flip], flip) for flip in flips], quad)
        quads = jnp.stack(quads, axis=0)
        layers = [quads] + [hop_layer(quads, flip) for flip in flips]
        layers = jnp.stack(turned(layers, layer_z), axis=0)
        twin = hop_core(layers)
        cores = jnp.stack([jnp.where(core == 0, layers, twin), jnp.where(core == 0, twin, layers)])
        packed = cores.reshape(width, PACK)
    group_weight = packed[:, : 3 * GROUP_COLS]
    side = packed[:, 3 * GROUP_COLS : 3 * GROUP_COLS + SIDE].astype(jnp.float32)
    vector_rows = side[:, :8].T
    up_bias_full = side[:, 8:VECS].reshape(devices, own_rows, ratio)
    up_bias_full = jnp.swapaxes(up_bias_full, 1, 2).reshape(1, hidden)
    (
        qbias_full,
        vbias_full,
        obias_full,
        again_full,
        ashift_full,
        dbias_full,
        fgain_full,
        fshift_full,
    ) = [vector_rows[number] for number in range(8)]
    docs = doc_lengths.shape[1]
    digits = side.reshape(2, width // 2, SIDE)[:, : groups * docs, VECS : VECS + 2]
    lengths_all = (digits[..., 0] * 64 + digits[..., 1]).astype(jnp.int32)
    lengths = lax.dynamic_index_in_dim(
        lengths_all.reshape(2 * groups, docs), layer_z, axis=0, keepdims=False
    )
    doc_ends = jnp.cumsum(lengths)

    def half_segments(which):
        turn_z = jnp.stack([(layer_z - turn) % 2 for turn in (0, 1)]) + 2 * which
        spot = jnp.stack([quad ^ flip for flip in range(4)])
        start = turn_z[None, :] * (4 * stretch) + spot[:, None] * stretch
        positions = start[:, :, None] + jnp.arange(stretch, dtype=jnp.int32)
        positions = positions.reshape(-1)
        return jnp.sum((positions[:, None] >= doc_ends[None, :]).astype(jnp.int32), axis=-1)

    seg_query = half_segments(core)
    seg_key = jnp.concatenate([seg_query, half_segments(1 - core)])
    seg_key = jnp.broadcast_to(seg_key[:, None], (seg_key.shape[0], 128))
    seg_query = seg_query[None, :]

    bulk = jnp.concatenate(
        [output_weight]
        + [up_weight[:, number * width : (number + 1) * width] for number in range(ratio)]
        + [down_weight],
        axis=0,
    )
    bulk_all = lax.all_gather(bulk, ("batch", "seq"), axis=0, tiled=True)
    bulk_all = bulk_all.reshape(devices, bulk_rows, width)

    with jax.named_scope("projections"):
        column_bias = jnp.concatenate(
            [
                jnp.zeros((GROUP_COLS,), jnp.float32),
                lax.dynamic_slice_in_dim(vbias_full, quad * GROUP_COLS, GROUP_COLS),
                lax.dynamic_slice_in_dim(qbias_full, quad * GROUP_COLS, GROUP_COLS),
            ]
        )
        projected = (matmul_plain(token_half, group_weight) + column_bias).astype(jnp.bfloat16)
        own_pair = projected[:, : 2 * GROUP_COLS]
        queries = projected[:, 2 * GROUP_COLS :]
        other_pair = hop_core(own_pair)
    ctx_wide, lse = attend(queries, own_pair, other_pair, seg_key, seg_query)

    with jax.named_scope("context_home"):
        ctx_blocks = ctx_wide.astype(jnp.bfloat16).reshape(4, row_count, GROUP_COLS)
        ctx_groups = [ctx_blocks[0]] + [hop_quad(ctx_blocks[flip], flip) for flip in flips]
        ctx_merged = jnp.concatenate(turned(ctx_groups, quad), axis=1)
        ctx_turns = [
            to_owner(ctx_merged[turn * stretch : (turn + 1) * stretch], turn) for turn in (0, 1)
        ]
        context_low = jnp.concatenate(
            [
                jnp.where(parity == 0, ctx_turns[0], ctx_turns[1]),
                jnp.where(parity == 0, ctx_turns[1], ctx_turns[0]),
            ],
            axis=0,
        )

    output_full = bulk_all[:, :own_rows].reshape(width, width)
    up_parts = [
        bulk_all[:, (1 + number) * own_rows : (2 + number) * own_rows].reshape(width, width)
        for number in range(ratio)
    ]
    up_full = jnp.concatenate(up_parts, axis=1)
    down_full = bulk_all[:, (1 + ratio) * own_rows :].reshape(hidden, width)

    token_rows = tokens.reshape(row_count, width)
    res_one = token_rows.astype(jnp.float32) + matmul_plain(context_low, output_full) + obias_full
    normed, pull_one = jax.vjp(norm_apply, res_one, again_full, ashift_full)
    normed_low = normed.astype(jnp.bfloat16)
    up_pre = matmul_plain(normed_low, up_full) + up_bias_full
    activated, pull_gelu = jax.vjp(gelu_exact, up_pre)
    act_low = activated.astype(jnp.bfloat16)
    res_two = normed + matmul_plain(act_low, down_full) + dbias_full
    output_rows, pull_two = jax.vjp(norm_apply, res_two, fgain_full, fshift_full)
    mixed = output_rows.astype(jnp.bfloat16).reshape(tokens.shape)
    grad_out = cotangent.astype(jnp.float32).reshape(row_count, width)
    grad_res_two, grad_ffn_gain, grad_ffn_shift = pull_two(grad_out)
    grad_down_low = grad_res_two.astype(jnp.bfloat16)
    (grad_up_pre,) = pull_gelu(matmul_right_t(grad_down_low, down_full))
    grad_up_low = grad_up_pre.astype(jnp.bfloat16)
    grad_normed = grad_res_two + matmul_right_t(grad_up_low, up_full)
    grad_res_one, grad_attn_gain, grad_attn_shift = pull_one(grad_normed)
    grad_branch_low = grad_res_one.astype(jnp.bfloat16)
    grad_context = matmul_right_t(grad_branch_low, output_full).astype(jnp.bfloat16)

    with jax.named_scope("context_grad_out"):
        low_part = grad_context[:stretch]
        high_part = grad_context[stretch:]
        grad_turns = [
            to_sequence(jnp.where((parity + turn) % 2 == 1, high_part, low_part), turn)
            for turn in (0, 1)
        ]
        grad_own = jnp.concatenate(grad_turns, axis=0)
        grad_columns = turned(
            [grad_own[:, n * GROUP_COLS : (n + 1) * GROUP_COLS] for n in range(4)], quad
        )
        grad_ctx = jnp.concatenate(
            [grad_columns[0]] + [hop_quad(grad_columns[flip], flip) for flip in flips], axis=0
        )

    def half_columns(matrix, which):
        half = matrix.shape[1] // 2
        return lax.dynamic_slice_in_dim(matrix, which * half, half, axis=1)

    def down_term(which):
        return matmul_left_t(half_columns(act_low, which), grad_down_low)

    def branch_term(which):
        return jnp.concatenate(
            [
                matmul_left_t(half_columns(normed_low, which), grad_up_low),
                matmul_left_t(half_columns(context_low, which), grad_branch_low),
            ],
            axis=1,
        )

    with jax.named_scope("down_grads"):
        sum_down = scatter_sum(down_term, ratio * own_rows, core, layer_z, quad)
    with jax.named_scope("branch_grads"):
        sum_branch = scatter_sum(branch_term, own_rows, core, layer_z, quad)
        sum_up = sum_branch[:, :hidden]
        sum_output = sum_branch[:, hidden:]

    grad_query, grad_own_pair, grad_other_pair = attend_back(
        queries, grad_ctx, ctx_wide, lse, own_pair, other_pair, seg_key, seg_query
    )
    with jax.named_scope("pair_sum"):
        arrived_pair = hop_core(grad_other_pair.astype(jnp.bfloat16)).astype(jnp.float32)
        pair_total = grad_own_pair + arrived_pair
        pair_scale = jnp.where(jnp.arange(2 * GROUP_COLS) < GROUP_COLS, SCALE, 1.0)
        grad_projected = jnp.concatenate([pair_total * pair_scale, grad_query], axis=1).astype(
            jnp.bfloat16
        )

    with jax.named_scope("token_grads"):
        grad_half = matmul_right_t(grad_projected, group_weight)
        half_blocks = grad_half.reshape(4, row_count, width)
        low_blocks = half_blocks.astype(jnp.bfloat16)
        grad_block = half_blocks[0]
        for flip in flips:
            grad_block = grad_block + hop_quad(low_blocks[flip], flip).astype(jnp.float32)
        grad_block = grad_block.astype(jnp.bfloat16)
        home = [
            to_owner(grad_block[turn * stretch : (turn + 1) * stretch], turn) for turn in (0, 1)
        ]
        home_rows = jnp.concatenate(
            [
                jnp.where(parity == 0, home[0], home[1]),
                jnp.where(parity == 0, home[1], home[0]),
            ],
            axis=0,
        )
        grad_tokens = (grad_res_one + home_rows.astype(jnp.float32)).reshape(tokens.shape)

    with jax.named_scope("group_weight_grads"):
        grad_group = matmul_left_t(token_half, grad_projected)
        bias_sums = column_sums(grad_projected)
        nothing = jnp.zeros((width,), jnp.float32)
        vec_rows = jnp.stack(
            [
                lax.dynamic_update_slice_in_dim(
                    nothing, bias_sums[2 * GROUP_COLS :], quad * GROUP_COLS, 0
                ),
                lax.dynamic_update_slice_in_dim(
                    nothing, bias_sums[GROUP_COLS : 2 * GROUP_COLS], quad * GROUP_COLS, 0
                ),
                column_sums(grad_branch_low),
                grad_attn_gain,
                grad_attn_shift,
                column_sums(grad_down_low),
                grad_ffn_gain,
                grad_ffn_shift,
            ],
            axis=0,
        ).T
        up_sums = column_sums(grad_up_low).reshape(devices, ratio, own_rows)
        up_sums = jnp.swapaxes(up_sums, 1, 2).reshape(width, ratio)
        vecs = jnp.concatenate([vec_rows, up_sums], axis=1)
        packed_grads = pack_grads(grad_group, vecs).reshape(2, width // 2, PACK)
        mine = jnp.where(core == 0, packed_grads[0], packed_grads[1])
        theirs = jnp.where(core == 0, packed_grads[1], packed_grads[0])
        main, vecs = unpack_grads(mine)
        more, more_vecs = unpack_grads(hop_core(theirs))
        main, vecs = (main + more, vecs + more_vecs)
        packed_grads = pack_grads(main, vecs).reshape(4, 4 * own_rows, PACK)
        by_layer = turned([packed_grads[number] for number in range(4)], layer_z)
        main, vecs = unpack_grads(by_layer[0])
        for flip in flips:
            more, more_vecs = unpack_grads(hop_layer(by_layer[flip], flip))
            main, vecs = (main + more, vecs + more_vecs)
        packed_grads = pack_grads(main, vecs).reshape(4, own_rows, PACK)
        by_quad = turned([packed_grads[number] for number in range(4)], quad)
        main, vecs = unpack_grads(by_quad[0])
        quad_parts = [main]
        for flip in flips:
            more, more_vecs = unpack_grads(hop_quad(by_quad[flip], flip))
            quad_parts.append(more)
            vecs = vecs + more_vecs
        quad_parts = turned(quad_parts, quad)
        sum_key, sum_value, sum_query = [
            jnp.concatenate([part[:, n * GROUP_COLS : (n + 1) * GROUP_COLS] for part in quad_parts], axis=1)
            for n in range(3)
        ]
    sum_rows = vecs[:, :8].T
    return (
        mixed,
        grad_tokens,
        sum_query,
        sum_rows[0],
        sum_key,
        sum_value,
        sum_rows[1],
        sum_output,
        sum_rows[2],
        sum_rows[3],
        sum_rows[4],
        sum_up,
        vecs[:, 8:].T.reshape(up_bias.shape),
        sum_down,
        sum_rows[5],
        sum_rows[6],
        sum_rows[7],
    )


def solution(mesh):
    in_specs = (
        P("batch", "seq", None),
        P("batch", None),
        P(("batch", "seq"), None),
        P(("batch", "seq")),
        P(("batch", "seq"), None),
        P(("batch", "seq"), None),
        P(("batch", "seq")),
        P(("batch", "seq"), None),
        P(("batch", "seq")),
        P(("batch", "seq")),
        P(("batch", "seq")),
        P(("batch", "seq"), None),
        P(("batch", "seq")),
        P(("batch", "seq"), None),
        P(("batch", "seq")),
        P(("batch", "seq")),
        P(("batch", "seq")),
        P("batch", "seq", None),
    )
    out_specs = (
        P("batch", "seq", None),
        P("batch", "seq", None),
        P(("batch", "seq"), None),
        P(("batch", "seq")),
        P(("batch", "seq"), None),
        P(("batch", "seq"), None),
        P(("batch", "seq")),
        P(("batch", "seq"), None),
        P(("batch", "seq")),
        P(("batch", "seq")),
        P(("batch", "seq")),
        P(("batch", "seq"), None),
        P(("batch", "seq")),
        P(("batch", "seq"), None),
        P(("batch", "seq")),
        P(("batch", "seq")),
        P(("batch", "seq")),
    )
    fits = mesh.shape['batch'] == 2 and mesh.shape['seq'] == 16
    body = shards_heads if fits else shards_general
    return jax.shard_map(body, mesh=mesh, in_specs=in_specs, out_specs=out_specs, check_vma=False)
```

profile of v0, /device:TPU:18, one launch (start us, length us, event | category | flops | bytes accessed | tf_op | source)
XLA Modules:
  0.0 370.6 jit_solution(1668785997262648368)
XLA Ops:
  20.7 2.8 collective-permute-start.1
  28.2 12.7 %collective-permute-done.10 = bf16[4,24,640]{2,1,0:T(8,128)(2,1)S(1)} collective-permute-done((bf16[4,24,640]{2,1,0:T(8,128)(2,1)S(1)}, bf16[4,24,640]{2,1,0:T(8,128)(2,1)S(1)}, u32[]{:S(2)}, u32[]{:S(2)}) %collective-permute-start.10) | collective-permute-done | bytes 122912 | tf_op jit(solution)/shard_map/group_weights/ppermute | solution.py:649
  40.9 5.9 %collective-permute-done.9 = bf16[4,24,640]{2,1,0:T(8,128)(2,1)S(1)} collective-permute-done((bf16[4,24,640]{2,1,0:T(8,128)(2,1)S(1)}, bf16[4,24,640]{2,1,0:T(8,128)(2,1)S(1)}, u32[]{:S(2)}, u32[]{:S(2)}) %collective-permute-start.9) | collective-permute-done | bytes 122912 | tf_op jit(solution)/shard_map/group_weights/ppermute | solution.py:649
  53.9 14.0 %collective-permute-done.2 = bf16[256,768]{1,0:T(8,128)(2,1)S(1)} collective-permute-done((bf16[256,768]{1,0:T(8,128)(2,1)S(1)}, bf16[256,768]{1,0:T(8,128)(2,1)S(1)}, u32[]{:S(2)}, u32[]{:S(2)}) %collective-permute-start.2) | collective-permute-done | bytes 393248 | tf_op jit(solution)/shard_map/tokens_out/ppermute | solution.py:649
  67.9 10.1 %collective-permute-done.4 = bf16[256,768]{1,0:T(8,128)(2,1)S(1)} collective-permute-done((bf16[256,768]{1,0:T(8,128)(2,1)S(1)}, bf16[256,768]{1,0:T(8,128)(2,1)S(1)}, u32[]{:S(2)}, u32[]{:S(2)}) %collective-permute-start.4) | collective-permute-done | bytes 393248 | tf_op jit(solution)/shard_map/tokens_out/ppermute | solution.py:649
  80.5 2.8 add_convert_fusion.2
  84.4 2.5 collective-permute-done.12.other_ref
  89.3 14.0 %attend.1 = (f32[1024,192]{1,0:T(8,128)S(1)}, f32[8,1024]{1,0:T(8,128)S(1)}) custom-call(bf16[1024,192]{1,0:T(8,128)(2,1)S(1)} %slice.468.query_ref, bf16[1024,384]{1,0:T(8,128)(2,1)S(1)} %slice.469.own_ref, bf16[1024,384]{1,0:T(8,128)(2,1)S(1)} %copy-done.1, s32[2048,128]{1,0:T(8,128)S(1)} %broadcast_in_dim.29.seg_key_ref, s32[1,1024]{1,0:T(1,128)S(1)} %bitcast.151), custom_call_target="tpu_custom_call" | custom-call | flops 3221225472 | bytes 4194304 | tf_op jit(solution)/shard_map/attend/pallas_call | solution.py:427
  108.4 3.1 collective-permute-done.15
  111.5 3.2 collective-permute-done.14
  122.6 2.9 collective-permute-done.16
  125.5 2.6 collective-permute-done.17
  129.9 2.6 slice.487
  132.6 3.2 fusion.76
  136.8 7.6 %multiply_convert_fusion = (bf16[256,3072]{1,0:T(8,128)(2,1)S(1)}, f32[256,3072]{1,0:T(8,128)S(1)}, f32[256,3072]{1,0:T(8,128)S(1)}) fusion(f32[3072]{0:T(1024)S(1)} %add.433, bf16[256,768]{1,0:T(8,128)(2,1)S(1)} %fusion.29, bf16[768,768]{1,0:T(8,128)(2,1)S(1)} %bitcast.170, bf16[768,768]{1,0:T(8,128)(2,1)S(1)} %bitcast.172, ...), kind=kOutput, calls=%fused_computation.11 | convolution fusion | flops 1278738432 | bytes 12988416 | tf_op jit(solution)/shard_map/dot_general | solution.py:34
  147.9 14.4 %convert_reduce_fusion = (f32[3072]{0:T(1024)S(1)}, bf16[256,3072]{1,0:T(8,128)(2,1)S(1)}) fusion(f32[256,3072]{1,0:T(8,128)S(1)} %get-tuple-element.79, f32[256,3072]{1,0:T(8,128)S(1)} %get-tuple-element.169, bf16[256,768]{1,0:T(8,128)(2,1)S(1)} %get-tuple-element.69, bf16[3072,768]{1,0:T(8,128)(2,1)S(1)} %bitcast.167), kind=kOutput, calls=%fused_computation.9 | convolution fusion | flops 1220539392 | bytes 12988416 | tf_op jit(solution)/shard_map/dot_general | solution.py:38
  168.0 4.7 %collective-permute-start.18 = (bf16[128,768]{1,0:T(8,128)(2,1)S(1)}, bf16[128,768]{1,0:T(8,128)(2,1)S(1)}, u32[]{:S(2)}, u32[]{:S(2)}) collective-permute-start(bf16[128,768]{1,0:T(8,128)(2,1)S(1)} %get-tuple-element.128), channel_id=1, source_target_pairs={{0,0},{1,1},{2,2},{3,3},{4,4},{5,5},{6,6},{7,7},{8,16},{9,17},{10,... | collective-permute-start | bytes 589832 | tf_op jit(solution)/shard_map/context_grad_out/ppermute | solution.py:649
  189.3 18.8 %attend_back.1 = (f32[1024,192]{1,0:T(8,128)S(1)}, f32[1024,384]{1,0:T(8,128)}, f32[1024,384]{1,0:T(8,128)}) custom-call(bf16[1024,192]{1,0:T(8,128)(2,1)S(1)} %slice.468.query_ref, bf16[1024,192]{1,0:T(8,128)(2,1)S(1)} %pad_maximum_fusion.6.grad_ref, f32[1024,192]{1,0:T(8,128)S(1)} %get-tuple-element.34.ctx_ref, f32[8,1024]{1,0:T(8,128)S(1)} %get-tuple-element.35.lse_ref, ...), custom_call_target="tpu_custom_call" | custom-call | flops 8053063680 | bytes 10485760 | tf_op jit(solution)/shard_map/attend_back/pallas_call | solution.py:516
  213.6 3.0 fusion.42
  222.9 4.1 %fusion.88 = (bf16[1024,768]{1,0:T(8,128)(2,1)S(1)}, f32[1024,768]{1,0:T(8,128)}) fusion(bf16[768,640]{1,0:T(8,128)(2,1)S(1)} %bitcast.163, bf16[1024,192]{1,0:T(8,128)(2,1)} %copy-done.13, bf16[1024,384]{1,0:T(8,128)(2,1)S(1)} %multiply_convert_fusion.1), kind=kOutput, calls=%fused_computation.301 | convolution fusion | flops 909115392 | bytes 6881280 | tf_op jit(solution)/shard_map/token_grads/dot_general | solution.py:38
  233.8 7.9 %collective-permute-done.24 = bf16[256,768]{1,0:T(8,128)(2,1)S(1)} collective-permute-done((bf16[256,768]{1,0:T(8,128)(2,1)S(1)}, bf16[256,768]{1,0:T(8,128)(2,1)S(1)}, u32[]{:S(2)}, u32[]{:S(2)}) %collective-permute-start.24) | collective-permute-done | bytes 393248 | tf_op jit(solution)/shard_map/token_grads/ppermute | solution.py:649
  241.7 8.4 %collective-permute-done.26 = bf16[256,768]{1,0:T(8,128)(2,1)S(1)} collective-permute-done((bf16[256,768]{1,0:T(8,128)(2,1)S(1)}, bf16[256,768]{1,0:T(8,128)(2,1)S(1)}, u32[]{:S(2)}, u32[]{:S(2)}) %collective-permute-start.26) | collective-permute-done | bytes 393248 | tf_op jit(solution)/shard_map/token_grads/ppermute | solution.py:649
  254.9 3.4 collective-permute-start.28
  262.1 11.0 %collective-permute-done.28 = bf16[128,768]{1,0:T(8,128)(2,1)S(1)} collective-permute-done((bf16[128,768]{1,0:T(8,128)(2,1)S(1)}, bf16[128,768]{1,0:T(8,128)(2,1)S(1)}, u32[]{:S(2)}, u32[]{:S(2)}) %collective-permute-start.28) | collective-permute-done | bytes 196640 | tf_op jit(solution)/shard_map/token_grads/ppermute | solution.py:649
  273.2 4.7 %collective-permute-done.32 = bf16[96,640]{1,0:T(8,128)(2,1)S(1)} collective-permute-done((bf16[96,640]{1,0:T(8,128)(2,1)S(1)}, bf16[96,640]{1,0:T(8,128)(2,1)S(1)}, u32[]{:S(2)}, u32[]{:S(2)}) %collective-permute-start.32) | collective-permute-done | bytes 122912 | tf_op jit(solution)/shard_map/group_weight_grads/ppermute | solution.py:649
  286.7 2.7 add_convert_fusion
  293.1 2.7 fusion
  298.3 7.6 %collective-permute-done.44 = bf16[4,96,768]{2,1,0:T(8,128)(2,1)S(1)} collective-permute-done((bf16[4,96,768]{2,1,0:T(8,128)(2,1)S(1)}, bf16[4,96,768]{2,1,0:T(8,128)(2,1)S(1)}, u32[]{:S(2)}, u32[]{:S(2)}) %collective-permute-start.44) | collective-permute-done | bytes 589856 | tf_op jit(solution)/shard_map/down_grads/ppermute | solution.py:649
  308.9 9.9 %collective-permute-done.46 = bf16[4,96,768]{2,1,0:T(8,128)(2,1)S(1)} collective-permute-done((bf16[4,96,768]{2,1,0:T(8,128)(2,1)S(1)}, bf16[4,96,768]{2,1,0:T(8,128)(2,1)S(1)}, u32[]{:S(2)}, u32[]{:S(2)}) %collective-permute-start.46) | collective-permute-done | bytes 589856 | tf_op jit(solution)/shard_map/down_grads/ppermute | solution.py:649
  321.3 13.1 %collective-permute-done.37 = bf16[4,24,3840]{2,1,0:T(8,128)(2,1)S(1)} collective-permute-done((bf16[4,24,3840]{2,1,0:T(8,128)(2,1)S(1)}, bf16[4,24,3840]{2,1,0:T(8,128)(2,1)S(1)}, u32[]{:S(2)}, u32[]{:S(2)}) %collective-permute-start.37) | collective-permute-done | bytes 737312 | tf_op jit(solution)/shard_map/branch_grads/ppermute | solution.py:649
  334.3 11.5 %collective-permute-done.39 = bf16[4,24,3840]{2,1,0:T(8,128)(2,1)S(1)} collective-permute-done((bf16[4,24,3840]{2,1,0:T(8,128)(2,1)S(1)}, bf16[4,24,3840]{2,1,0:T(8,128)(2,1)S(1)}, u32[]{:S(2)}, u32[]{:S(2)}) %collective-permute-start.39) | collective-permute-done | bytes 737312 | tf_op jit(solution)/shard_map/branch_grads/ppermute | solution.py:649
  355.2 6.8 %collective-permute-done.42 = bf16[24,3840]{1,0:T(8,128)(2,1)S(1)} collective-permute-done((bf16[24,3840]{1,0:T(8,128)(2,1)S(1)}, bf16[24,3840]{1,0:T(8,128)(2,1)S(1)}, u32[]{:S(2)}, u32[]{:S(2)}) %collective-permute-start.42) | collective-permute-done | bytes 184352 | tf_op jit(solution)/shard_map/branch_grads/ppermute | solution.py:649
  (316 shorter events, 130.6 us)
Async XLA Ops:
  7.2 122.7 %all-gather.2.cloned.1.call-start = ((), (), s32[]{:S(2)}) async-start(), calls=%async_computation | async-start | bytes 10948608 | tf_op jit(solution)/shard_map/all_gather | solution.py:815
  18.8 29.4 %collective-permute-start = (bf16[128,768]{1,0:T(8,128)(2,1)}, bf16[128,768]{1,0:T(8,128)(2,1)S(1)}, u32[]{:S(2)}, u32[]{:S(2)}) collective-permute-start(bf16[128,768]{1,0:T(8,128)(2,1)} %get-tuple-element.28), channel_id=1, source_target_pairs={{0,0},{1,1},{2,2},{3,3},{4,4},{5,5},{6,6},{7,7},{8,16},{9,17},{10,... | collective-permute-start | bytes 589832 | tf_op jit(solution)/shard_map/tokens_out/ppermute | solution.py:649
  20.7 27.5 %collective-permute-start.1 = (bf16[128,768]{1,0:T(8,128)(2,1)}, bf16[128,768]{1,0:T(8,128)(2,1)S(1)}, u32[]{:S(2)}, u32[]{:S(2)}) collective-permute-start(bf16[128,768]{1,0:T(8,128)(2,1)} %get-tuple-element.29), channel_id=1, source_target_pairs={{0,4},{1,5},{2,6},{3,7},{4,0},{5,1},{6,2},{7,3},{8,20},{9,21},{10,... | collective-permute-start | bytes 589832 | tf_op jit(solution)/shard_map/tokens_out/ppermute | solution.py:649
  24.5 16.3 %collective-permute-start.10 = (bf16[4,24,640]{2,1,0:T(8,128)(2,1)S(1)}, bf16[4,24,640]{2,1,0:T(8,128)(2,1)S(1)}, u32[]{:S(2)}, u32[]{:S(2)}) collective-permute-start(bf16[4,24,640]{2,1,0:T(8,128)(2,1)S(1)} %pad_maximum_fusion.13), channel_id=1, source_target_pairs={{0,4},{1,5},{2,6},{3,7},{4,0},{5,1},{6,2},{7,3},{8,12},{9,13},{10,... | collective-permute-start | bytes 368648 | tf_op jit(solution)/shard_map/group_weights/ppermute | solution.py:649
  25.9 20.8 %collective-permute-start.9 = (bf16[4,24,640]{2,1,0:T(8,128)(2,1)S(1)}, bf16[4,24,640]{2,1,0:T(8,128)(2,1)S(1)}, u32[]{:S(2)}, u32[]{:S(2)}) collective-permute-start(bf16[4,24,640]{2,1,0:T(8,128)(2,1)S(1)} %pad_maximum_fusion.13), channel_id=1, source_target_pairs={{0,8},{1,9},{2,10},{3,11},{4,12},{5,13},{6,14},{7,15},{8,0},{9,1},... | collective-permute-start | bytes 368648 | tf_op jit(solution)/shard_map/group_weights/ppermute | solution.py:649
  25.9 22.1 %collective-permute-start.8 = (bf16[4,24,640]{2,1,0:T(8,128)(2,1)S(1)}, bf16[4,24,640]{2,1,0:T(8,128)(2,1)S(1)}, u32[]{:S(2)}, u32[]{:S(2)}) collective-permute-start(bf16[4,24,640]{2,1,0:T(8,128)(2,1)S(1)} %pad_maximum_fusion.13), channel_id=1, source_target_pairs={{0,12},{1,13},{2,14},{3,15},{4,8},{5,9},{6,10},{7,11},{8,4},{9,5},... | collective-permute-start | bytes 368648 | tf_op jit(solution)/shard_map/group_weights/ppermute | solution.py:649
  48.3 19.6 %collective-permute-start.2 = (bf16[256,768]{1,0:T(8,128)(2,1)S(1)}, bf16[256,768]{1,0:T(8,128)(2,1)S(1)}, u32[]{:S(2)}, u32[]{:S(2)}) collective-permute-start(bf16[256,768]{1,0:T(8,128)(2,1)S(1)} %get-tuple-element.137), channel_id=1, source_target_pairs={{0,1},{1,0},{2,3},{3,2},{4,5},{5,4},{6,7},{7,6},{8,9},{9,8},{10,11... | collective-permute-start | bytes 1179656 | tf_op jit(solution)/shard_map/tokens_out/ppermute | solution.py:649
  48.8 19.0 %collective-permute-start.3 = (bf16[256,768]{1,0:T(8,128)(2,1)S(1)}, bf16[256,768]{1,0:T(8,128)(2,1)S(1)}, u32[]{:S(2)}, u32[]{:S(2)}) collective-permute-start(bf16[256,768]{1,0:T(8,128)(2,1)S(1)} %get-tuple-element.137), channel_id=1, source_target_pairs={{0,2},{1,3},{2,0},{3,1},{4,6},{5,7},{6,4},{7,5},{8,10},{9,11},{10,... | collective-permute-start | bytes 1179656 | tf_op jit(solution)/shard_map/tokens_out/ppermute | solution.py:649
  50.6 28.6 %collective-permute-start.11 = (bf16[4,4,24,640]{3,2,1,0:T(8,128)(2,1)S(1)}, bf16[4,4,24,640]{3,2,1,0:T(8,128)(2,1)S(1)}, u32[]{:S(2)}, u32[]{:S(2)}) collective-permute-start(bf16[4,4,24,640]{3,2,1,0:T(8,128)(2,1)S(1)} %pad_maximum_fusion.8), channel_id=1, source_target_pairs={{0,16},{1,17},{2,18},{3,19},{4,20},{5,21},{6,22},{7,23},{8,24},{9,... | collective-permute-start | bytes 1474568 | tf_op jit(solution)/shard_map/group_weights/ppermute | solution.py:649
  52.3 25.7 %collective-permute-start.4 = (bf16[256,768]{1,0:T(8,128)(2,1)S(1)}, bf16[256,768]{1,0:T(8,128)(2,1)S(1)}, u32[]{:S(2)}, u32[]{:S(2)}) collective-permute-start(bf16[256,768]{1,0:T(8,128)(2,1)S(1)} %get-tuple-element.137), channel_id=1, source_target_pairs={{0,3},{1,2},{2,1},{3,0},{4,7},{5,6},{6,5},{7,4},{8,11},{9,10},{10,... | collective-permute-start | bytes 1179656 | tf_op jit(solution)/shard_map/tokens_out/ppermute | solution.py:649
  166.0 11.5 %collective-permute-start.19 = (bf16[128,768]{1,0:T(8,128)(2,1)S(1)}, bf16[128,768]{1,0:T(8,128)(2,1)S(1)}, u32[]{:S(2)}, u32[]{:S(2)}) collective-permute-start(bf16[128,768]{1,0:T(8,128)(2,1)S(1)} %get-tuple-element.127), channel_id=1, source_target_pairs={{0,4},{1,5},{2,6},{3,7},{4,0},{5,1},{6,2},{7,3},{8,20},{9,21},{10,... | collective-permute-start | bytes 589832 | tf_op jit(solution)/shard_map/context_grad_out/ppermute | solution.py:649
  168.0 9.5 %collective-permute-start.18 = (bf16[128,768]{1,0:T(8,128)(2,1)S(1)}, bf16[128,768]{1,0:T(8,128)(2,1)S(1)}, u32[]{:S(2)}, u32[]{:S(2)}) collective-permute-start(bf16[128,768]{1,0:T(8,128)(2,1)S(1)} %get-tuple-element.128), channel_id=1, source_target_pairs={{0,0},{1,1},{2,2},{3,3},{4,4},{5,5},{6,6},{7,7},{8,16},{9,17},{10,... | collective-permute-start | bytes 589832 | tf_op jit(solution)/shard_map/context_grad_out/ppermute | solution.py:649
  184.9 101.7 %collective-permute-start.43 = (bf16[1536,768]{1,0:T(8,128)(2,1)}, bf16[1536,768]{1,0:T(8,128)(2,1)}, u32[]{:S(2)}, u32[]{:S(2)}) collective-permute-start(bf16[1536,768]{1,0:T(8,128)(2,1)} %convolution_convert_fusion.1), channel_id=1, source_target_pairs={{0,16},{1,17},{2,18},{3,19},{4,20},{5,21},{6,22},{7,23},{8,24},{9,... | collective-permute-start | bytes 7077896 | tf_op jit(solution)/shard_map/down_grads/ppermute | solution.py:649
  212.1 81.0 %collective-permute-start.36 = (bf16[384,3840]{1,0:T(8,128)(2,1)}, bf16[384,3840]{1,0:T(8,128)(2,1)}, u32[]{:S(2)}, u32[]{:S(2)}) collective-permute-start(bf16[384,3840]{1,0:T(8,128)(2,1)} %pad_maximum_fusion.1), channel_id=1, source_target_pairs={{0,16},{1,17},{2,18},{3,19},{4,20},{5,21},{6,22},{7,23},{8,24},{9,... | collective-permute-start | bytes 8847368 | tf_op jit(solution)/shard_map/branch_grads/ppermute | solution.py:649
  229.7 12.0 %collective-permute-start.24 = (bf16[256,768]{1,0:T(8,128)(2,1)S(1)}, bf16[256,768]{1,0:T(8,128)(2,1)S(1)}, u32[]{:S(2)}, u32[]{:S(2)}) collective-permute-start(bf16[256,768]{1,0:T(8,128)(2,1)S(1)} %get-tuple-element.91), channel_id=1, source_target_pairs={{0,1},{1,0},{2,3},{3,2},{4,5},{5,4},{6,7},{7,6},{8,9},{9,8},{10,11... | collective-permute-start | bytes 1179656 | tf_op jit(solution)/shard_map/token_grads/ppermute | solution.py:649
  230.3 19.8 %collective-permute-start.26 = (bf16[256,768]{1,0:T(8,128)(2,1)S(1)}, bf16[256,768]{1,0:T(8,128)(2,1)S(1)}, u32[]{:S(2)}, u32[]{:S(2)}) collective-permute-start(bf16[256,768]{1,0:T(8,128)(2,1)S(1)} %get-tuple-element.92), channel_id=1, source_target_pairs={{0,3},{1,2},{2,1},{3,0},{4,7},{5,6},{6,5},{7,4},{8,11},{9,10},{10,... | collective-permute-start | bytes 1179656 | tf_op jit(solution)/shard_map/token_grads/ppermute | solution.py:649
  232.2 19.2 %collective-permute-start.25 = (bf16[256,768]{1,0:T(8,128)(2,1)S(1)}, bf16[256,768]{1,0:T(8,128)(2,1)S(1)}, u32[]{:S(2)}, u32[]{:S(2)}) collective-permute-start(bf16[256,768]{1,0:T(8,128)(2,1)S(1)} %get-tuple-element.93), channel_id=1, source_target_pairs={{0,2},{1,3},{2,0},{3,1},{4,6},{5,7},{6,4},{7,5},{8,10},{9,11},{10,... | collective-permute-start | bytes 1179656 | tf_op jit(solution)/shard_map/token_grads/ppermute | solution.py:649
  241.7 16.6 %collective-permute-start.29 = (bf16[384,640]{1,0:T(8,128)(2,1)S(1)}, bf16[384,640]{1,0:T(8,128)(2,1)S(1)}, u32[]{:S(2)}, u32[]{:S(2)}) collective-permute-start(bf16[384,640]{1,0:T(8,128)(2,1)S(1)} %get-tuple-element.95), channel_id=1, source_target_pairs={{0,16},{1,17},{2,18},{3,19},{4,20},{5,21},{6,22},{7,23},{8,24},{9,... | collective-permute-start | bytes 1474568 | tf_op jit(solution)/shard_map/group_weight_grads/ppermute | solution.py:649
  254.9 18.2 %collective-permute-start.28 = (bf16[128,768]{1,0:T(8,128)(2,1)S(1)}, bf16[128,768]{1,0:T(8,128)(2,1)S(1)}, u32[]{:S(2)}, u32[]{:S(2)}) collective-permute-start(bf16[128,768]{1,0:T(8,128)(2,1)S(1)} %get-tuple-element.122), channel_id=1, source_target_pairs={{0,4},{1,5},{2,6},{3,7},{4,0},{5,1},{6,2},{7,3},{8,20},{9,21},{10,... | collective-permute-start | bytes 589832 | tf_op jit(solution)/shard_map/token_grads/ppermute | solution.py:649
  259.0 14.1 %collective-permute-start.30 = (bf16[96,640]{1,0:T(8,128)(2,1)S(1)}, bf16[96,640]{1,0:T(8,128)(2,1)S(1)}, u32[]{:S(2)}, u32[]{:S(2)}) collective-permute-start(bf16[96,640]{1,0:T(8,128)(2,1)S(1)} %get-tuple-element.113), channel_id=1, source_target_pairs={{0,4},{1,5},{2,6},{3,7},{4,0},{5,1},{6,2},{7,3},{8,12},{9,13},{10,... | collective-permute-start | bytes 368648 | tf_op jit(solution)/shard_map/group_weight_grads/ppermute | solution.py:649
  262.1 11.1 %collective-permute-start.31 = (bf16[96,640]{1,0:T(8,128)(2,1)S(1)}, bf16[96,640]{1,0:T(8,128)(2,1)S(1)}, u32[]{:S(2)}, u32[]{:S(2)}) collective-permute-start(bf16[96,640]{1,0:T(8,128)(2,1)S(1)} %get-tuple-element.114), channel_id=1, source_target_pairs={{0,8},{1,9},{2,10},{3,11},{4,12},{5,13},{6,14},{7,15},{8,0},{9,1},... | collective-permute-start | bytes 368648 | tf_op jit(solution)/shard_map/group_weight_grads/ppermute | solution.py:649
  289.5 16.3 %collective-permute-start.44 = (bf16[4,96,768]{2,1,0:T(8,128)(2,1)S(1)}, bf16[4,96,768]{2,1,0:T(8,128)(2,1)S(1)}, u32[]{:S(2)}, u32[]{:S(2)}) collective-permute-start(bf16[4,96,768]{2,1,0:T(8,128)(2,1)S(1)} %get-tuple-element.88), channel_id=1, source_target_pairs={{0,1},{1,0},{2,3},{3,2},{4,5},{5,4},{6,7},{7,6},{8,9},{9,8},{10,11... | collective-permute-start | bytes 1769480 | tf_op jit(solution)/shard_map/down_grads/ppermute | solution.py:649
  290.6 28.1 %collective-permute-start.46 = (bf16[4,96,768]{2,1,0:T(8,128)(2,1)S(1)}, bf16[4,96,768]{2,1,0:T(8,128)(2,1)S(1)}, u32[]{:S(2)}, u32[]{:S(2)}) collective-permute-start(bf16[4,96,768]{2,1,0:T(8,128)(2,1)S(1)} %get-tuple-element.89), channel_id=1, source_target_pairs={{0,3},{1,2},{2,1},{3,0},{4,7},{5,6},{6,5},{7,4},{8,11},{9,10},{10,... | collective-permute-start | bytes 1769480 | tf_op jit(solution)/shard_map/down_grads/ppermute | solution.py:649
  291.8 28.4 %collective-permute-start.45 = (bf16[4,96,768]{2,1,0:T(8,128)(2,1)S(1)}, bf16[4,96,768]{2,1,0:T(8,128)(2,1)S(1)}, u32[]{:S(2)}, u32[]{:S(2)}) collective-permute-start(bf16[4,96,768]{2,1,0:T(8,128)(2,1)S(1)} %get-tuple-element.90), channel_id=1, source_target_pairs={{0,2},{1,3},{2,0},{3,1},{4,6},{5,7},{6,4},{7,5},{8,10},{9,11},{10,... | collective-permute-start | bytes 1769480 | tf_op jit(solution)/shard_map/down_grads/ppermute | solution.py:649
  296.0 38.4 %collective-permute-start.37 = (bf16[4,24,3840]{2,1,0:T(8,128)(2,1)S(1)}, bf16[4,24,3840]{2,1,0:T(8,128)(2,1)S(1)}, u32[]{:S(2)}, u32[]{:S(2)}) collective-permute-start(bf16[4,24,3840]{2,1,0:T(8,128)(2,1)S(1)} %get-tuple-element.85), channel_id=1, source_target_pairs={{0,1},{1,0},{2,3},{3,2},{4,5},{5,4},{6,7},{7,6},{8,9},{9,8},{10,11... | collective-permute-start | bytes 2211848 | tf_op jit(solution)/shard_map/branch_grads/ppermute | solution.py:649
  297.1 48.6 %collective-permute-start.39 = (bf16[4,24,3840]{2,1,0:T(8,128)(2,1)S(1)}, bf16[4,24,3840]{2,1,0:T(8,128)(2,1)S(1)}, u32[]{:S(2)}, u32[]{:S(2)}) collective-permute-start(bf16[4,24,3840]{2,1,0:T(8,128)(2,1)S(1)} %get-tuple-element.86), channel_id=1, source_target_pairs={{0,3},{1,2},{2,1},{3,0},{4,7},{5,6},{6,5},{7,4},{8,11},{9,10},{10,... | collective-permute-start | bytes 2211848 | tf_op jit(solution)/shard_map/branch_grads/ppermute | solution.py:649
  305.8 41.3 %collective-permute-start.38 = (bf16[4,24,3840]{2,1,0:T(8,128)(2,1)S(1)}, bf16[4,24,3840]{2,1,0:T(8,128)(2,1)S(1)}, u32[]{:S(2)}, u32[]{:S(2)}) collective-permute-start(bf16[4,24,3840]{2,1,0:T(8,128)(2,1)S(1)} %get-tuple-element.87), channel_id=1, source_target_pairs={{0,2},{1,3},{2,0},{3,1},{4,6},{5,7},{6,4},{7,5},{8,10},{9,11},{10,... | collective-permute-start | bytes 2211848 | tf_op jit(solution)/shard_map/branch_grads/ppermute | solution.py:649
  320.5 29.7 %collective-permute-start.47 = (bf16[96,768]{1,0:T(8,128)(2,1)S(1)}, bf16[96,768]{1,0:T(8,128)(2,1)S(1)}, u32[]{:S(2)}, u32[]{:S(2)}) collective-permute-start(bf16[96,768]{1,0:T(8,128)(2,1)S(1)} %get-tuple-element.106), channel_id=1, source_target_pairs={{0,4},{1,5},{2,6},{3,7},{4,0},{5,1},{6,2},{7,3},{8,12},{9,13},{10,... | collective-permute-start | bytes 442376 | tf_op jit(solution)/shard_map/down_grads/ppermute | solution.py:649
  320.6 31.4 %collective-permute-start.49 = (bf16[96,768]{1,0:T(8,128)(2,1)S(1)}, bf16[96,768]{1,0:T(8,128)(2,1)S(1)}, u32[]{:S(2)}, u32[]{:S(2)}) collective-permute-start(bf16[96,768]{1,0:T(8,128)(2,1)S(1)} %get-tuple-element.107), channel_id=1, source_target_pairs={{0,12},{1,13},{2,14},{3,15},{4,8},{5,9},{6,10},{7,11},{8,4},{9,5},... | collective-permute-start | bytes 442376 | tf_op jit(solution)/shard_map/down_grads/ppermute | solution.py:649
  334.3 17.7 %collective-permute-start.48 = (bf16[96,768]{1,0:T(8,128)(2,1)S(1)}, bf16[96,768]{1,0:T(8,128)(2,1)S(1)}, u32[]{:S(2)}, u32[]{:S(2)}) collective-permute-start(bf16[96,768]{1,0:T(8,128)(2,1)S(1)} %get-tuple-element.108), channel_id=1, source_target_pairs={{0,8},{1,9},{2,10},{3,11},{4,12},{5,13},{6,14},{7,15},{8,0},{9,1},... | collective-permute-start | bytes 442376 | tf_op jit(solution)/shard_map/down_grads/ppermute | solution.py:649
  348.3 13.7 %collective-permute-start.42 = (bf16[24,3840]{1,0:T(8,128)(2,1)S(1)}, bf16[24,3840]{1,0:T(8,128)(2,1)S(1)}, u32[]{:S(2)}, u32[]{:S(2)}) collective-permute-start(bf16[24,3840]{1,0:T(8,128)(2,1)S(1)} %get-tuple-element.104), channel_id=1, source_target_pairs={{0,12},{1,13},{2,14},{3,15},{4,8},{5,9},{6,10},{7,11},{8,4},{9,5},... | collective-permute-start | bytes 552968 | tf_op jit(solution)/shard_map/branch_grads/ppermute | solution.py:649
  350.2 11.9 %collective-permute-start.41 = (bf16[24,3840]{1,0:T(8,128)(2,1)S(1)}, bf16[24,3840]{1,0:T(8,128)(2,1)S(1)}, u32[]{:S(2)}, u32[]{:S(2)}) collective-permute-start(bf16[24,3840]{1,0:T(8,128)(2,1)S(1)} %get-tuple-element.105), channel_id=1, source_target_pairs={{0,8},{1,9},{2,10},{3,11},{4,12},{5,13},{6,14},{7,15},{8,0},{9,1},... | collective-permute-start | bytes 552968 | tf_op jit(solution)/shard_map/branch_grads/ppermute | solution.py:649
  (56 other events, 398.5 us)
Sparse Core Ops, SparseCore 0:
  12.9 105.7 all-gather.1
where the time goes:
time: 376 us; the launch traced here: 371 us
  waiting for transfers between devices  152 us (40%)
  starting transfers between devices  59.1 us (16%)
  matrix products  48 us (13%)
  Pallas kernels  35.3 us (9%)
  local copies, waits for them, and re-layouts  33.7 us (9%)
  other arithmetic  27 us (7%)
  between operations  15.5 us (4%)
    ppermute x50, waiting for transfers between devices, hop(): return lax.ppermute(value, ('batch', 'seq'), device_table(mapping))  152 us
    ppermute x50, starting transfers between devices, hop(): return lax.ppermute(value, ('batch', 'seq'), device_table(mapping))  59.1 us
    dot_general x4, matrix products, matmul_right_t(): lax.dot_general(left_op, right_op, (((1,), (1,)), ((), ())), preferred_el...  20.7 us
    pallas_call x1, Pallas kernels, attend_back(): pl.pallas_call(attend_back_kernel, grid=(4,), in_specs=[pl.BlockSpec((blo...  18.8 us
    dot_general x7, matrix products, matmul_left_t(): lax.dot_general(left_op, right_op, (((0,), (0,)), ((), ())), preferred_el...  14.8 us
    pallas_call x1, Pallas kernels, attend(): pl.pallas_call(attend_kernel, grid=(4,), in_specs=[pl.BlockSpec((block, G...  14 us
    unnamed x84, local copies, waits for them, and re-layouts  12.5 us
    dot_general x4, matrix products, matmul_plain(): return jnp.dot(left_op, right_op, preferred_element_type=jnp.float32)  12.5 us
  transfers between devices with their start and end apart: 51, of which 30 were waited for; matrix products, arithmetic and copies ran while one was open for 16% of the time, Pallas kernels for 10%

commit v1 on v0

--- a/solution.py
+++ b/solution.py
@@ -539,9 +539,7 @@
         scratch_shapes=[pltpu.VMEM((GROUP_COLS, 2 * half), jnp.bfloat16)],
         compiler_params=pltpu.CompilerParams(vmem_limit_bytes=48 * 1024 * 1024),
         cost_estimate=pl.CostEstimate(
-            flops=40 * rows * half * GROUP_COLS,
-            bytes_accessed=10 * 1024 * 1024,
-            transcendentals=2 * GROUP_HEADS * rows * half,
+            flops=rows * half * GROUP_COLS, bytes_accessed=1024 * 1024, transcendentals=0
         ),
         name="attend_back",
     )(query, grad, ctx, lse, own, other, seg_key, seg_query)
@@ -562,8 +560,12 @@
     fgain_ref,
     fshift_ref,
     ubias_ref,
+    output_ref,
+    up_ref,
+    down_ref,
     first_ref,
     second_ref,
+    bulk_ref,
     *piece_refs,
 ):
     place = lax.axis_index("seq")
@@ -571,7 +573,14 @@
     quad = lax.rem(place, 4)
     first_ref[...] = jnp.where(odd, tokens_ref[1], tokens_ref[0])
     second_ref[...] = jnp.where(odd, tokens_ref[0], tokens_ref[1])
-    own_rows = key_ref.shape[0]
+    own_rows, width = key_ref.shape
+    ratio = up_ref.shape[1] // width
+    bulk_ref[0, :own_rows] = output_ref[...]
+    for number in range(ratio):
+        bulk_ref[0, (1 + number) * own_rows : (2 + number) * own_rows] = up_ref[
+            :, number * width : (number + 1) * width
+        ]
+    bulk_ref[0, (1 + ratio) * own_rows :] = down_ref[...]
     small = (qbias_ref, vbias_ref, obias_ref, again_ref, ashift_ref, dbias_ref, fgain_ref, fshift_ref)
     rows = [ref[...].astype(jnp.float32) for ref in small]
     wide = ubias_ref[...].astype(jnp.float32)
@@ -598,13 +607,16 @@
                     piece_ref[:, spot * GROUP_COLS : (spot + 1) * GROUP_COLS] = ref[:, cols]
 
 
-def prepare(tokens, lengths, key, value, query, vectors, up_bias):
-    own_rows = key.shape[0]
+def prepare(tokens, lengths, key, value, query, vectors, up_bias, output, up, down):
+    own_rows, width = key.shape
+    bulk_rows = own_rows + down.shape[0] * 2
     turn_shape = jax.ShapeDtypeStruct(tokens.shape[1:], jnp.bfloat16)
     piece_shape = jax.ShapeDtypeStruct((own_rows, PACK), jnp.bfloat16)
     return pl.pallas_call(
         prepare_kernel,
-        out_shape=[turn_shape] * 2 + [piece_shape] * 4,
+        out_shape=[turn_shape] * 2
+        + [jax.ShapeDtypeStruct((1, bulk_rows, width), jnp.bfloat16)]
+        + [piece_shape] * 4,
         name="prepare",
     )(
         tokens,
@@ -614,25 +626,32 @@
         query,
         *[item.reshape(1, own_rows) for item in vectors],
         up_bias.reshape(1, up_bias.shape[0]),
-    )
-
-
-def scatter_sum(term, rows, core, layer_z, quad):
-    theirs = term(1 - core).astype(jnp.bfloat16)
-    total = (term(core) + hop_core(theirs).astype(jnp.float32)).astype(jnp.bfloat16)
-    blocks = total.reshape(4, 4, rows, total.shape[-1])
-
-    def block(values, index, axis):
-        return lax.dynamic_index_in_dim(values, index, axis=axis, keepdims=False)
-
-    part = block(blocks, quad, 1).astype(jnp.float32)
-    for flip in (1, 2, 3):
-        part = part + hop_quad(block(blocks, quad ^ flip, 1), flip).astype(jnp.float32)
-    blocks = part.astype(jnp.bfloat16)
-    part = block(part, layer_z, 0)
-    for flip in (1, 2, 3):
-        part = part + hop_layer(block(blocks, layer_z ^ flip, 0), flip).astype(jnp.float32)
-    return part
+        output,
+        up,
+        down,
+    )
+
+
+def tied(values, *others):
+    return lax.optimization_barrier((values, others))[0]
+
+
+def block_of(values, index, axis):
+    return lax.dynamic_index_in_dim(values, index, axis=axis, keepdims=False)
+
+
+def split_blocks(values, place, axis):
+    low = values.astype(jnp.bfloat16)
+    return [block_of(values, place, axis)] + [
+        block_of(low, place ^ flip, axis) for flip in (1, 2, 3)
+    ]
+
+
+def sum_parts(own, arrived):
+    total = own.astype(jnp.float32)
+    for item in arrived:
+        total = total + item.astype(jnp.float32)
+    return total
 
 
 def device_table(mapping):
@@ -750,8 +769,17 @@
         ffn_gain,
         ffn_shift,
     )
-    first_turn, second_turn, *pieces = prepare(
-        tokens, doc_lengths, key_weight, value_weight, query_weight, vectors, up_bias
+    first_turn, second_turn, bulk, *pieces = prepare(
+        tokens,
+        doc_lengths,
+        key_weight,
+        value_weight,
+        query_weight,
+        vectors,
+        up_bias,
+        output_weight,
+        up_weight,
+        down_weight,
     )
 
     with jax.named_scope("tokens_out"):
@@ -806,14 +834,7 @@
     seg_key = jnp.broadcast_to(seg_key[:, None], (seg_key.shape[0], 128))
     seg_query = seg_query[None, :]
 
-    bulk = jnp.concatenate(
-        [output_weight]
-        + [up_weight[:, number * width : (number + 1) * width] for number in range(ratio)]
-        + [down_weight],
-        axis=0,
-    )
     bulk_all = lax.all_gather(bulk, ("batch", "seq"), axis=0, tiled=True)
-    bulk_all = bulk_all.reshape(devices, bulk_rows, width)
 
     with jax.named_scope("projections"):
         column_bias = jnp.concatenate(
@@ -865,12 +886,34 @@
     grad_out = cotangent.astype(jnp.float32).reshape(row_count, width)
     grad_res_two, grad_ffn_gain, grad_ffn_shift = pull_two(grad_out)
     grad_down_low = grad_res_two.astype(jnp.bfloat16)
-    (grad_up_pre,) = pull_gelu(matmul_right_t(grad_down_low, down_full))
+
+    def half_columns(matrix, which):
+        half = matrix.shape[1] // 2
+        return lax.dynamic_slice_in_dim(matrix, which * half, half, axis=1)
+
+    def down_term(which):
+        return matmul_left_t(half_columns(act_low, which), grad_down_low)
+
+    def branch_term(which):
+        return jnp.concatenate(
+            [
+                matmul_left_t(half_columns(normed_low, which), grad_up_low),
+                matmul_left_t(half_columns(context_low, which), grad_branch_low),
+            ],
+            axis=1,
+        )
+
+    with jax.named_scope("down_grads"):
+        down_theirs = down_term(1 - core).astype(jnp.bfloat16)
+        down_arrived = hop_core(down_theirs)
+    (grad_up_pre,) = pull_gelu(matmul_right_t(tied(grad_down_low, down_theirs), down_full))
     grad_up_low = grad_up_pre.astype(jnp.bfloat16)
     grad_normed = grad_res_two + matmul_right_t(grad_up_low, up_full)
     grad_res_one, grad_attn_gain, grad_attn_shift = pull_one(grad_normed)
     grad_branch_low = grad_res_one.astype(jnp.bfloat16)
     grad_context = matmul_right_t(grad_branch_low, output_full).astype(jnp.bfloat16)
+    with jax.named_scope("branch_grads"):
+        branch_arrived = hop_core(branch_term(1 - core).astype(jnp.bfloat16))
 
     with jax.named_scope("context_grad_out"):
         low_part = grad_context[:stretch]
@@ -887,59 +930,37 @@
             [grad_columns[0]] + [hop_quad(grad_columns[flip], flip) for flip in flips], axis=0
         )
 
-    def half_columns(matrix, which):
-        half = matrix.shape[1] // 2
-        return lax.dynamic_slice_in_dim(matrix, which * half, half, axis=1)
-
-    def down_term(which):
-        return matmul_left_t(half_columns(act_low, which), grad_down_low)
-
-    def branch_term(which):
-        return jnp.concatenate(
-            [
-                matmul_left_t(half_columns(normed_low, which), grad_up_low),
-                matmul_left_t(half_columns(context_low, which), grad_branch_low),
-            ],
-            axis=1,
-        )
-
     with jax.named_scope("down_grads"):
-        sum_down = scatter_sum(down_term, ratio * own_rows, core, layer_z, quad)
+        down_total = (down_term(core) + down_arrived.astype(jnp.float32)).astype(jnp.bfloat16)
+        down_blocks = down_total.reshape(4, 4, ratio * own_rows, width)
+        down_quads = tied(split_blocks(down_blocks, quad, 1), grad_ctx)
     with jax.named_scope("branch_grads"):
-        sum_branch = scatter_sum(branch_term, own_rows, core, layer_z, quad)
-        sum_up = sum_branch[:, :hidden]
-        sum_output = sum_branch[:, hidden:]
+        branch_total = (branch_term(core) + branch_arrived.astype(jnp.float32)).astype(jnp.bfloat16)
+        branch_blocks = branch_total.reshape(4, 4, own_rows, hidden + width)
+        branch_quads = split_blocks(branch_blocks, quad, 1)
+    with jax.named_scope("down_grads"):
+        down_arrived = [hop_quad(down_quads[flip], flip) for flip in flips]
 
     grad_query, grad_own_pair, grad_other_pair = attend_back(
-        queries, grad_ctx, ctx_wide, lse, own_pair, other_pair, seg_key, seg_query
+        tied(queries, down_quads, branch_quads),
+        grad_ctx,
+        ctx_wide,
+        lse,
+        own_pair,
+        other_pair,
+        seg_key,
+        seg_query,
     )
     with jax.named_scope("pair_sum"):
         arrived_pair = hop_core(grad_other_pair.astype(jnp.bfloat16)).astype(jnp.float32)
+        branch_quads = tied(branch_quads, arrived_pair, down_arrived)
         pair_total = grad_own_pair + arrived_pair
         pair_scale = jnp.where(jnp.arange(2 * GROUP_COLS) < GROUP_COLS, SCALE, 1.0)
         grad_projected = jnp.concatenate([pair_total * pair_scale, grad_query], axis=1).astype(
             jnp.bfloat16
         )
-
-    with jax.named_scope("token_grads"):
-        grad_half = matmul_right_t(grad_projected, group_weight)
-        half_blocks = grad_half.reshape(4, row_count, width)
-        low_blocks = half_blocks.astype(jnp.bfloat16)
-        grad_block = half_blocks[0]
-        for flip in flips:
-            grad_block = grad_block + hop_quad(low_blocks[flip], flip).astype(jnp.float32)
-        grad_block = grad_block.astype(jnp.bfloat16)
-        home = [
-            to_owner(grad_block[turn * stretch : (turn + 1) * stretch], turn) for turn in (0, 1)
-        ]
-        home_rows = jnp.concatenate(
-            [
-                jnp.where(parity == 0, home[0], home[1]),
-                jnp.where(parity == 0, home[1], home[0]),
-            ],
-            axis=0,
-        )
-        grad_tokens = (grad_res_one + home_rows.astype(jnp.float32)).reshape(tokens.shape)
+    with jax.named_scope("branch_grads"):
+        branch_arrived = [hop_quad(branch_quads[flip], flip) for flip in flips]
 
     with jax.named_scope("group_weight_grads"):
         grad_group = matmul_left_t(token_half, grad_projected)
@@ -973,6 +994,25 @@
         main, vecs = (main + more, vecs + more_vecs)
         packed_grads = pack_grads(main, vecs).reshape(4, 4 * own_rows, PACK)
         by_layer = turned([packed_grads[number] for number in range(4)], layer_z)
+
+    with jax.named_scope("token_grads"):
+        grad_half = matmul_right_t(grad_projected, group_weight)
+        half_blocks = grad_half.reshape(4, row_count, width)
+        low_blocks = half_blocks.astype(jnp.bfloat16)
+        down_part = sum_parts(down_quads[0], tied(down_arrived, low_blocks))
+        down_layers = split_blocks(down_part, layer_z, 0)
+        down_arrived = [hop_layer(down_layers[flip], flip) for flip in flips]
+        grad_block = half_blocks[0]
+        for flip in flips:
+            grad_block = grad_block + hop_quad(low_blocks[flip], flip).astype(jnp.float32)
+        grad_block = grad_block.astype(jnp.bfloat16)
+        branch_part = sum_parts(branch_quads[0], tied(branch_arrived, grad_block))
+        branch_layers = split_blocks(branch_part, layer_z, 0)
+        branch_arrived = [hop_layer(branch_layers[flip], flip) for flip in flips]
+        grad_block = tied(grad_block, branch_layers, by_layer, down_layers)
+        home = [
+            to_owner(grad_block[turn * stretch : (turn + 1) * stretch], turn) for turn in (0, 1)
+        ]
         main, vecs = unpack_grads(by_layer[0])
         for flip in flips:
             more, more_vecs = unpack_grads(hop_layer(by_layer[flip], flip))
@@ -980,6 +1020,17 @@
         packed_grads = pack_grads(main, vecs).reshape(4, own_rows, PACK)
         by_quad = turned([packed_grads[number] for number in range(4)], quad)
         main, vecs = unpack_grads(by_quad[0])
+        by_quad = tied(by_quad, home, branch_arrived)
+        home_rows = jnp.concatenate(
+            [
+                jnp.where(parity == 0, home[0], home[1]),
+                jnp.where(parity == 0, home[1], home[0]),
+            ],
+            axis=0,
+        )
+        grad_tokens = (grad_res_one + home_rows.astype(jnp.float32)).reshape(tokens.shape)
+
+    with jax.named_scope("group_weight_grads"):
         quad_parts = [main]
         for flip in flips:
             more, more_vecs = unpack_grads(hop_quad(by_quad[flip], flip))
@@ -991,6 +1042,10 @@
             for n in range(3)
         ]
     sum_rows = vecs[:, :8].T
+    sum_down = sum_parts(down_layers[0], down_arrived)
+    sum_branch = sum_parts(branch_layers[0], branch_arrived)
+    sum_up = sum_branch[:, :hidden]
+    sum_output = sum_branch[:, hidden:]
     return (
         mixed,
         grad_tokens,

time: 376 us -> 383 us (1.019)
  matrix products: 48 us -> 30.7 us
  starting transfers between devices: 59.1 us -> 66.6 us
  other arithmetic: 27 us -> 33.9 us
  local copies, waits for them, and re-layouts: 33.7 us -> 40.4 us
    dot_general x4, matrix products: 20.7 us -> 8.36 us  [matmul_right_t(): lax.dot_general(left_op, right_op, (((1,), (1,)), ((), ())), preferred_el...]
    ppermute x50, starting transfers between devices: 59.1 us -> 66.5 us  [hop(): return lax.ppermute(value, ('batch', 'seq'), device_table(mapping))]
    dot_general x7, matrix products: 14.8 us -> 9.91 us  [matmul_left_t(): lax.dot_general(left_op, right_op, (((0,), (0,)), ((), ())), preferred_el...]
    unnamed x84 -> x95, local copies, waits for them, and re-layouts: 12.5 us -> 8.81 us
  transfers between devices with their start and end apart: 51 -> 51, of which waited for: 30 -> 31; matrix products, arithmetic and copies ran while one was open for 16% -> 17% of each run, Pallas kernels for 10% -> 4%
where the time goes in v1:
time: 383 us; the launch traced here: 376 us
  waiting for transfers between devices  153 us (40%)
  starting transfers between devices  66.6 us (17%)
  local copies, waits for them, and re-layouts  40.4 us (11%)
  Pallas kernels  35.8 us (9%)
  other arithmetic  33.9 us (9%)
  matrix products  30.7 us (8%)
  between operations  15.7 us (4%)
    ppermute x50, waiting for transfers between devices, hop(): return lax.ppermute(value, ('batch', 'seq'), device_table(mapping))  152 us
    ppermute x50, starting transfers between devices, hop(): return lax.ppermute(value, ('batch', 'seq'), device_table(mapping))  66.5 us
    pallas_call x1, Pallas kernels, attend_back(): pl.pallas_call(attend_back_kernel, grid=(4,), in_specs=[pl.BlockSpec((blo...  19 us
    pallas_call x1, Pallas kernels, attend(): pl.pallas_call(attend_kernel, grid=(4,), in_specs=[pl.BlockSpec((block, G...  14 us
    dot_general x4, matrix products, matmul_plain(): return jnp.dot(left_op, right_op, preferred_element_type=jnp.float32)  12.4 us
    dot_general x7, matrix products, matmul_left_t(): lax.dot_general(left_op, right_op, (((0,), (0,)), ((), ())), preferred_el...  9.91 us
    unnamed x95, local copies, waits for them, and re-layouts  8.81 us
    dot_general x4, matrix products, matmul_right_t(): lax.dot_general(left_op, right_op, (((1,), (1,)), ((), ())), preferred_el...  8.36 us
  transfers between devices with their start and end apart: 51, of which 31 were waited for; matrix products, arithmetic and copies ran while one was open for 17% of the time, Pallas kernels for 4%

profile of v1, /device:TPU:18, one launch (start us, length us, event | category | flops | bytes accessed | tf_op | source)
XLA Modules:
  0.0 376.3 jit_solution(15691007188669786678)
XLA Ops:
  7.2 2.7 prepare.1
  15.5 2.8 collective-permute-start.1
  22.9 10.1 %collective-permute-done.10 = bf16[4,24,640]{2,1,0:T(8,128)(2,1)S(1)} collective-permute-done((bf16[4,24,640]{2,1,0:T(8,128)(2,1)S(1)}, bf16[4,24,640]{2,1,0:T(8,128)(2,1)S(1)}, u32[]{:S(2)}, u32[]{:S(2)}) %collective-permute-start.10) | collective-permute-done | bytes 122912 | tf_op jit(solution)/shard_map/group_weights/ppermute | solution.py:668
  33.0 8.5 %collective-permute-done.9 = bf16[4,24,640]{2,1,0:T(8,128)(2,1)S(1)} collective-permute-done((bf16[4,24,640]{2,1,0:T(8,128)(2,1)S(1)}, bf16[4,24,640]{2,1,0:T(8,128)(2,1)S(1)}, u32[]{:S(2)}, u32[]{:S(2)}) %collective-permute-start.9) | collective-permute-done | bytes 122912 | tf_op jit(solution)/shard_map/group_weights/ppermute | solution.py:668
  49.0 10.2 %collective-permute-done.2 = bf16[256,768]{1,0:T(8,128)(2,1)S(1)} collective-permute-done((bf16[256,768]{1,0:T(8,128)(2,1)S(1)}, bf16[256,768]{1,0:T(8,128)(2,1)S(1)}, u32[]{:S(2)}, u32[]{:S(2)}) %collective-permute-start.2) | collective-permute-done | bytes 393248 | tf_op jit(solution)/shard_map/tokens_out/ppermute | solution.py:668
  60.0 13.1 %collective-permute-done.4 = bf16[256,768]{1,0:T(8,128)(2,1)S(1)} collective-permute-done((bf16[256,768]{1,0:T(8,128)(2,1)S(1)}, bf16[256,768]{1,0:T(8,128)(2,1)S(1)}, u32[]{:S(2)}, u32[]{:S(2)}) %collective-permute-start.4) | collective-permute-done | bytes 393248 | tf_op jit(solution)/shard_map/tokens_out/ppermute | solution.py:668
  75.6 2.8 add_convert_fusion.2
  84.2 14.0 %attend.1 = (f32[1024,192]{1,0:T(8,128)S(1)}, f32[8,1024]{1,0:T(8,128)S(1)}) custom-call(bf16[1024,192]{1,0:T(8,128)(2,1)S(1)} %slice.452.query_ref, bf16[1024,384]{1,0:T(8,128)(2,1)S(1)} %slice.453.own_ref, bf16[1024,384]{1,0:T(8,128)(2,1)S(1)} %copy-done.2, s32[2048,128]{1,0:T(8,128)S(1)} %broadcast_in_dim.29.seg_key_ref, s32[1,1024]{1,0:T(1,128)S(1)} %bitcast.140), custom_call_target="tpu_custom_call" | custom-call | flops 3221225472 | bytes 4194304 | tf_op jit(solution)/shard_map/attend/pallas_call | solution.py:427
  101.9 3.3 collective-permute-done.15
  116.2 6.5 %collective-permute-done.16 = bf16[128,768]{1,0:T(8,128)(2,1)} collective-permute-done((bf16[128,768]{1,0:T(8,128)(2,1)}, bf16[128,768]{1,0:T(8,128)(2,1)}, u32[]{:S(2)}, u32[]{:S(2)}) %collective-permute-start.16) | collective-permute-done | bytes 196640 | tf_op jit(solution)/shard_map/context_home/ppermute | solution.py:668
  122.7 2.9 collective-permute-done.17
  128.5 3.2 fusion.68
  133.7 7.6 %multiply_convert_fusion = (bf16[256,3072]{1,0:T(8,128)(2,1)S(1)}, f32[256,3072]{1,0:T(8,128)S(1)}, f32[256,3072]{1,0:T(8,128)S(1)}) fusion(f32[3072]{0:T(1024)S(1)} %add.433, bf16[256,768]{1,0:T(8,128)(2,1)S(1)} %fusion.25, bf16[768,768]{1,0:T(8,128)(2,1)S(1)} %bitcast.153, bf16[768,768]{1,0:T(8,128)(2,1)S(1)} %bitcast.155, ...), kind=kOutput, calls=%fused_computation.11 | convolution fusion | flops 1278738432 | bytes 12988416 | tf_op jit(solution)/shard_map/dot_general | solution.py:34
  141.3 3.2 slice.471
  150.8 2.7 convert_reduce_fusion
  162.9 4.2 %collective-permute-start.19 = (bf16[128,768]{1,0:T(8,128)(2,1)S(1)}, bf16[128,768]{1,0:T(8,128)(2,1)S(1)}, u32[]{:S(2)}, u32[]{:S(2)}) collective-permute-start(bf16[128,768]{1,0:T(8,128)(2,1)S(1)} %get-tuple-element.181), channel_id=1, source_target_pairs={{0,0},{1,1},{2,2},{3,3},{4,4},{5,5},{6,6},{7,7},{8,16},{9,17},{10,... | collective-permute-start | bytes 589832 | tf_op jit(solution)/shard_map/context_grad_out/ppermute | solution.py:668
  167.2 6.7 %collective-permute-done.19 = bf16[128,768]{1,0:T(8,128)(2,1)S(1)} collective-permute-done((bf16[128,768]{1,0:T(8,128)(2,1)S(1)}, bf16[128,768]{1,0:T(8,128)(2,1)S(1)}, u32[]{:S(2)}, u32[]{:S(2)}) %collective-permute-start.19) | collective-permute-done | bytes 196640 | tf_op jit(solution)/shard_map/context_grad_out/ppermute | solution.py:668
  184.0 3.2 collective-permute-done.23
  188.4 2.9 add_convert_fusion
  196.3 7.0 %collective-permute-done.29 = bf16[4,96,768]{2,1,0:T(8,128)(2,1)S(1)} collective-permute-done((bf16[4,96,768]{2,1,0:T(8,128)(2,1)S(1)}, bf16[4,96,768]{2,1,0:T(8,128)(2,1)S(1)}, u32[]{:S(2)}, u32[]{:S(2)}) %collective-permute-start.29) | collective-permute-done | bytes 589856 | tf_op jit(solution)/shard_map/down_grads/ppermute | solution.py:668
  203.3 8.1 %collective-permute-done.30 = bf16[4,96,768]{2,1,0:T(8,128)(2,1)S(1)} collective-permute-done((bf16[4,96,768]{2,1,0:T(8,128)(2,1)S(1)}, bf16[4,96,768]{2,1,0:T(8,128)(2,1)S(1)}, u32[]{:S(2)}, u32[]{:S(2)}) %collective-permute-start.30) | collective-permute-done | bytes 589856 | tf_op jit(solution)/shard_map/down_grads/ppermute | solution.py:668
  217.3 19.0 %attend_back.1 = (f32[1024,192]{1,0:T(8,128)S(1)}, f32[1024,384]{1,0:T(8,128)}, f32[1024,384]{1,0:T(8,128)}) custom-call(bf16[1024,192]{1,0:T(8,128)(2,1)S(1)} %slice.452.query_ref, bf16[1024,192]{1,0:T(8,128)(2,1)S(1)} %pad_maximum_fusion.6.grad_ref, f32[1024,192]{1,0:T(8,128)S(1)} %get-tuple-element.55.ctx_ref, f32[8,1024]{1,0:T(8,128)S(1)} %get-tuple-element.63.lse_ref, ...), custom_call_target="tpu_custom_call" | custom-call | flops 201326592 | bytes 1048576 | tf_op jit(solution)/shard_map/attend_back/pallas_call | solution.py:516
  236.3 2.8 convert_element_type.242
  240.2 3.5 collective-permute-start.49
  278.4 20.5 %collective-permute-done.26 = bf16[256,768]{1,0:T(8,128)(2,1)} collective-permute-done((bf16[256,768]{1,0:T(8,128)(2,1)}, bf16[256,768]{1,0:T(8,128)(2,1)}, u32[]{:S(2)}, u32[]{:S(2)}) %collective-permute-start.26) | collective-permute-done | bytes 393248 | tf_op jit(solution)/shard_map/token_grads/ppermute | solution.py:668
  301.4 4.5 %collective-permute-done.28 = bf16[256,768]{1,0:T(8,128)(2,1)S(1)} collective-permute-done((bf16[256,768]{1,0:T(8,128)(2,1)}, bf16[256,768]{1,0:T(8,128)(2,1)S(1)}, u32[]{:S(2)}, u32[]{:S(2)}) %collective-permute-start.28) | collective-permute-done | bytes 393248 | tf_op jit(solution)/shard_map/token_grads/ppermute | solution.py:668
  305.9 8.3 %collective-permute-done.27 = bf16[256,768]{1,0:T(8,128)(2,1)S(1)} collective-permute-done((bf16[256,768]{1,0:T(8,128)(2,1)}, bf16[256,768]{1,0:T(8,128)(2,1)S(1)}, u32[]{:S(2)}, u32[]{:S(2)}) %collective-permute-start.27) | collective-permute-done | bytes 393248 | tf_op jit(solution)/shard_map/token_grads/ppermute | solution.py:668
  326.2 9.1 %collective-permute-done.43 = bf16[24,3840]{1,0:T(8,128)(2,1)S(1)} collective-permute-done((bf16[24,3840]{1,0:T(8,128)(2,1)S(1)}, bf16[24,3840]{1,0:T(8,128)(2,1)S(1)}, u32[]{:S(2)}, u32[]{:S(2)}) %collective-permute-start.43) | collective-permute-done | bytes 184352 | tf_op jit(solution)/shard_map/token_grads/ppermute | solution.py:668
  335.3 6.0 %collective-permute-done.42 = bf16[24,3840]{1,0:T(8,128)(2,1)S(1)} collective-permute-done((bf16[24,3840]{1,0:T(8,128)(2,1)S(1)}, bf16[24,3840]{1,0:T(8,128)(2,1)S(1)}, u32[]{:S(2)}, u32[]{:S(2)}) %collective-permute-start.42) | collective-permute-done | bytes 184352 | tf_op jit(solution)/shard_map/token_grads/ppermute | solution.py:668
  344.8 4.1 %collective-permute-start.37 = (bf16[128,768]{1,0:T(8,128)(2,1)S(1)}, bf16[128,768]{1,0:T(8,128)(2,1)S(1)}, u32[]{:S(2)}, u32[]{:S(2)}) collective-permute-start(bf16[128,768]{1,0:T(8,128)(2,1)S(1)} %get-tuple-element.175), channel_id=1, source_target_pairs={{0,4},{1,5},{2,6},{3,7},{4,0},{5,1},{6,2},{7,3},{8,20},{9,21},{10,... | collective-permute-start | bytes 589832 | tf_op jit(solution)/shard_map/token_grads/ppermute | solution.py:668
  349.3 3.5 collective-permute-done.36
  352.8 4.9 %collective-permute-done.37 = bf16[128,768]{1,0:T(8,128)(2,1)S(1)} collective-permute-done((bf16[128,768]{1,0:T(8,128)(2,1)S(1)}, bf16[128,768]{1,0:T(8,128)(2,1)S(1)}, u32[]{:S(2)}, u32[]{:S(2)}) %collective-permute-start.37) | collective-permute-done | bytes 196640 | tf_op jit(solution)/shard_map/token_grads/ppermute | solution.py:668
  (325 shorter events, 148.7 us)
Async XLA Ops:
  7.2 121.3 %all-gather.2.cloned.1.call-start = ((), (), s32[]{:S(2)}) async-start(), calls=%async_computation | async-start | bytes 10948608 | tf_op jit(solution)/shard_map/all_gather | solution.py:837
  13.6 29.8 %collective-permute-start = (bf16[128,768]{1,0:T(8,128)(2,1)}, bf16[128,768]{1,0:T(8,128)(2,1)S(1)}, u32[]{:S(2)}, u32[]{:S(2)}) collective-permute-start(bf16[128,768]{1,0:T(8,128)(2,1)} %get-tuple-element.49), channel_id=1, source_target_pairs={{0,0},{1,1},{2,2},{3,3},{4,4},{5,5},{6,6},{7,7},{8,16},{9,17},{10,... | collective-permute-start | bytes 589832 | tf_op jit(solution)/shard_map/tokens_out/ppermute | solution.py:668
  15.5 28.0 %collective-permute-start.1 = (bf16[128,768]{1,0:T(8,128)(2,1)}, bf16[128,768]{1,0:T(8,128)(2,1)S(1)}, u32[]{:S(2)}, u32[]{:S(2)}) collective-permute-start(bf16[128,768]{1,0:T(8,128)(2,1)} %get-tuple-element.50), channel_id=1, source_target_pairs={{0,4},{1,5},{2,6},{3,7},{4,0},{5,1},{6,2},{7,3},{8,20},{9,21},{10,... | collective-permute-start | bytes 589832 | tf_op jit(solution)/shard_map/tokens_out/ppermute | solution.py:668
  19.3 13.7 %collective-permute-start.10 = (bf16[4,24,640]{2,1,0:T(8,128)(2,1)S(1)}, bf16[4,24,640]{2,1,0:T(8,128)(2,1)S(1)}, u32[]{:S(2)}, u32[]{:S(2)}) collective-permute-start(bf16[4,24,640]{2,1,0:T(8,128)(2,1)S(1)} %pad_maximum_fusion.13), channel_id=1, source_target_pairs={{0,4},{1,5},{2,6},{3,7},{4,0},{5,1},{6,2},{7,3},{8,12},{9,13},{10,... | collective-permute-start | bytes 368648 | tf_op jit(solution)/shard_map/group_weights/ppermute | solution.py:668
  20.7 20.8 %collective-permute-start.9 = (bf16[4,24,640]{2,1,0:T(8,128)(2,1)S(1)}, bf16[4,24,640]{2,1,0:T(8,128)(2,1)S(1)}, u32[]{:S(2)}, u32[]{:S(2)}) collective-permute-start(bf16[4,24,640]{2,1,0:T(8,128)(2,1)S(1)} %pad_maximum_fusion.13), channel_id=1, source_target_pairs={{0,8},{1,9},{2,10},{3,11},{4,12},{5,13},{6,14},{7,15},{8,0},{9,1},... | collective-permute-start | bytes 368648 | tf_op jit(solution)/shard_map/group_weights/ppermute | solution.py:668
  20.7 22.6 %collective-permute-start.8 = (bf16[4,24,640]{2,1,0:T(8,128)(2,1)S(1)}, bf16[4,24,640]{2,1,0:T(8,128)(2,1)S(1)}, u32[]{:S(2)}, u32[]{:S(2)}) collective-permute-start(bf16[4,24,640]{2,1,0:T(8,128)(2,1)S(1)} %pad_maximum_fusion.13), channel_id=1, source_target_pairs={{0,12},{1,13},{2,14},{3,15},{4,8},{5,9},{6,10},{7,11},{8,4},{9,5},... | collective-permute-start | bytes 368648 | tf_op jit(solution)/shard_map/group_weights/ppermute | solution.py:668
  43.5 15.7 %collective-permute-start.2 = (bf16[256,768]{1,0:T(8,128)(2,1)S(1)}, bf16[256,768]{1,0:T(8,128)(2,1)S(1)}, u32[]{:S(2)}, u32[]{:S(2)}) collective-permute-start(bf16[256,768]{1,0:T(8,128)(2,1)S(1)} %get-tuple-element.190), channel_id=1, source_target_pairs={{0,1},{1,0},{2,3},{3,2},{4,5},{5,4},{6,7},{7,6},{8,9},{9,8},{10,11... | collective-permute-start | bytes 1179656 | tf_op jit(solution)/shard_map/tokens_out/ppermute | solution.py:668
  44.1 15.9 %collective-permute-start.3 = (bf16[256,768]{1,0:T(8,128)(2,1)S(1)}, bf16[256,768]{1,0:T(8,128)(2,1)S(1)}, u32[]{:S(2)}, u32[]{:S(2)}) collective-permute-start(bf16[256,768]{1,0:T(8,128)(2,1)S(1)} %get-tuple-element.190), channel_id=1, source_target_pairs={{0,2},{1,3},{2,0},{3,1},{4,6},{5,7},{6,4},{7,5},{8,10},{9,11},{10,... | collective-permute-start | bytes 1179656 | tf_op jit(solution)/shard_map/tokens_out/ppermute | solution.py:668
  45.8 28.6 %collective-permute-start.11 = (bf16[4,4,24,640]{3,2,1,0:T(8,128)(2,1)S(1)}, bf16[4,4,24,640]{3,2,1,0:T(8,128)(2,1)S(1)}, u32[]{:S(2)}, u32[]{:S(2)}) collective-permute-start(bf16[4,4,24,640]{3,2,1,0:T(8,128)(2,1)S(1)} %pad_maximum_fusion.8), channel_id=1, source_target_pairs={{0,16},{1,17},{2,18},{3,19},{4,20},{5,21},{6,22},{7,23},{8,24},{9,... | collective-permute-start | bytes 1474568 | tf_op jit(solution)/shard_map/group_weights/ppermute | solution.py:668
  47.5 25.7 %collective-permute-start.4 = (bf16[256,768]{1,0:T(8,128)(2,1)S(1)}, bf16[256,768]{1,0:T(8,128)(2,1)S(1)}, u32[]{:S(2)}, u32[]{:S(2)}) collective-permute-start(bf16[256,768]{1,0:T(8,128)(2,1)S(1)} %get-tuple-element.190), channel_id=1, source_target_pairs={{0,3},{1,2},{2,1},{3,0},{4,7},{5,6},{6,5},{7,4},{8,11},{9,10},{10,... | collective-permute-start | bytes 1179656 | tf_op jit(solution)/shard_map/tokens_out/ppermute | solution.py:668
  111.8 13.7 %collective-permute-start.17 = (bf16[128,768]{1,0:T(8,128)(2,1)}, bf16[128,768]{1,0:T(8,128)(2,1)}, u32[]{:S(2)}, u32[]{:S(2)}) collective-permute-start(bf16[128,768]{1,0:T(8,128)(2,1)} %get-tuple-element.185), channel_id=1, source_target_pairs={{0,4},{1,5},{2,6},{3,7},{4,0},{5,1},{6,2},{7,3},{8,20},{9,21},{10,... | collective-permute-start | bytes 589832 | tf_op jit(solution)/shard_map/context_home/ppermute | solution.py:668
  150.5 37.9 %collective-permute-start.18 = (bf16[1536,768]{1,0:T(8,128)(2,1)}, bf16[1536,768]{1,0:T(8,128)(2,1)}, u32[]{:S(2)}, u32[]{:S(2)}) collective-permute-start(bf16[1536,768]{1,0:T(8,128)(2,1)} %convolution_convert_fusion.1), channel_id=1, source_target_pairs={{0,16},{1,17},{2,18},{3,19},{4,20},{5,21},{6,22},{7,23},{8,24},{9,... | collective-permute-start | bytes 7077896 | tf_op jit(solution)/shard_map/down_grads/ppermute | solution.py:668
  160.7 52.4 %collective-permute-start.24 = (bf16[384,3840]{1,0:T(8,128)(2,1)}, bf16[384,3840]{1,0:T(8,128)(2,1)}, u32[]{:S(2)}, u32[]{:S(2)}) collective-permute-start(bf16[384,3840]{1,0:T(8,128)(2,1)} %pad_maximum_fusion.1), channel_id=1, source_target_pairs={{0,16},{1,17},{2,18},{3,19},{4,20},{5,21},{6,22},{7,23},{8,24},{9,... | collective-permute-start | bytes 8847368 | tf_op jit(solution)/shard_map/branch_grads/ppermute | solution.py:668
  191.6 19.8 %collective-permute-start.30 = (bf16[4,96,768]{2,1,0:T(8,128)(2,1)S(1)}, bf16[4,96,768]{2,1,0:T(8,128)(2,1)S(1)}, u32[]{:S(2)}, u32[]{:S(2)}) collective-permute-start(bf16[4,96,768]{2,1,0:T(8,128)(2,1)S(1)} %get-tuple-element.60), channel_id=1, source_target_pairs={{0,2},{1,3},{2,0},{3,1},{4,6},{5,7},{6,4},{7,5},{8,10},{9,11},{10,... | collective-permute-start | bytes 1769480 | tf_op jit(solution)/shard_map/down_grads/ppermute | solution.py:668
  192.8 18.6 %collective-permute-start.31 = (bf16[4,96,768]{2,1,0:T(8,128)(2,1)S(1)}, bf16[4,96,768]{2,1,0:T(8,128)(2,1)S(1)}, u32[]{:S(2)}, u32[]{:S(2)}) collective-permute-start(bf16[4,96,768]{2,1,0:T(8,128)(2,1)S(1)} %get-tuple-element.61), channel_id=1, source_target_pairs={{0,3},{1,2},{2,1},{3,0},{4,7},{5,6},{6,5},{7,4},{8,11},{9,10},{10,... | collective-permute-start | bytes 1769480 | tf_op jit(solution)/shard_map/down_grads/ppermute | solution.py:668
  239.1 21.1 %collective-permute-start.25 = (bf16[1024,384]{1,0:T(8,128)(2,1)}, bf16[1024,384]{1,0:T(8,128)(2,1)S(1)}, u32[]{:S(2)}, u32[]{:S(2)}) collective-permute-start(bf16[1024,384]{1,0:T(8,128)(2,1)} %convert_element_type.242), channel_id=1, source_target_pairs={{0,16},{1,17},{2,18},{3,19},{4,20},{5,21},{6,22},{7,23},{8,24},{9,... | collective-permute-start | bytes 2359304 | tf_op jit(solution)/shard_map/pair_sum/ppermute | solution.py:668
  240.2 15.5 %collective-permute-start.47 = (bf16[96,768]{1,0:T(8,128)(2,1)}, bf16[96,768]{1,0:T(8,128)(2,1)}, u32[]{:S(2)}, u32[]{:S(2)}) collective-permute-start(bf16[96,768]{1,0:T(8,128)(2,1)} %get-tuple-element.158), channel_id=1, source_target_pairs={{0,4},{1,5},{2,6},{3,7},{4,0},{5,1},{6,2},{7,3},{8,12},{9,13},{10,... | collective-permute-start | bytes 442376 | tf_op jit(solution)/shard_map/token_grads/ppermute | solution.py:668
  240.2 16.4 %collective-permute-start.49 = (bf16[96,768]{1,0:T(8,128)(2,1)}, bf16[96,768]{1,0:T(8,128)(2,1)}, u32[]{:S(2)}, u32[]{:S(2)}) collective-permute-start(bf16[96,768]{1,0:T(8,128)(2,1)} %get-tuple-element.159), channel_id=1, source_target_pairs={{0,12},{1,13},{2,14},{3,15},{4,8},{5,9},{6,10},{7,11},{8,4},{9,5},... | collective-permute-start | bytes 442376 | tf_op jit(solution)/shard_map/token_grads/ppermute | solution.py:668
  243.7 14.7 %collective-permute-start.48 = (bf16[96,768]{1,0:T(8,128)(2,1)}, bf16[96,768]{1,0:T(8,128)(2,1)}, u32[]{:S(2)}, u32[]{:S(2)}) collective-permute-start(bf16[96,768]{1,0:T(8,128)(2,1)} %get-tuple-element.160), channel_id=1, source_target_pairs={{0,8},{1,9},{2,10},{3,11},{4,12},{5,13},{6,14},{7,15},{8,0},{9,1},... | collective-permute-start | bytes 442376 | tf_op jit(solution)/shard_map/token_grads/ppermute | solution.py:668
  254.8 60.6 %collective-permute-start.32 = (bf16[4,24,3840]{2,1,0:T(8,128)(2,1)}, bf16[4,24,3840]{2,1,0:T(8,128)(2,1)}, u32[]{:S(2)}, u32[]{:S(2)}) collective-permute-start(bf16[4,24,3840]{2,1,0:T(8,128)(2,1)} %get-tuple-element.68), channel_id=1, source_target_pairs={{0,1},{1,0},{2,3},{3,2},{4,5},{5,4},{6,7},{7,6},{8,9},{9,8},{10,11... | collective-permute-start | bytes 2211848 | tf_op jit(solution)/shard_map/branch_grads/ppermute | solution.py:668
  255.8 59.7 %collective-permute-start.33 = (bf16[4,24,3840]{2,1,0:T(8,128)(2,1)}, bf16[4,24,3840]{2,1,0:T(8,128)(2,1)}, u32[]{:S(2)}, u32[]{:S(2)}) collective-permute-start(bf16[4,24,3840]{2,1,0:T(8,128)(2,1)} %get-tuple-element.69), channel_id=1, source_target_pairs={{0,2},{1,3},{2,0},{3,1},{4,6},{5,7},{6,4},{7,5},{8,10},{9,11},{10,... | collective-permute-start | bytes 2211848 | tf_op jit(solution)/shard_map/branch_grads/ppermute | solution.py:668
  256.6 58.8 %collective-permute-start.34 = (bf16[4,24,3840]{2,1,0:T(8,128)(2,1)}, bf16[4,24,3840]{2,1,0:T(8,128)(2,1)}, u32[]{:S(2)}, u32[]{:S(2)}) collective-permute-start(bf16[4,24,3840]{2,1,0:T(8,128)(2,1)} %get-tuple-element.70), channel_id=1, source_target_pairs={{0,3},{1,2},{2,1},{3,0},{4,7},{5,6},{6,5},{7,4},{8,11},{9,10},{10,... | collective-permute-start | bytes 2211848 | tf_op jit(solution)/shard_map/branch_grads/ppermute | solution.py:668
  266.2 32.7 %collective-permute-start.26 = (bf16[256,768]{1,0:T(8,128)(2,1)}, bf16[256,768]{1,0:T(8,128)(2,1)}, u32[]{:S(2)}, u32[]{:S(2)}) collective-permute-start(bf16[256,768]{1,0:T(8,128)(2,1)} %get-tuple-element.143), channel_id=1, source_target_pairs={{0,1},{1,0},{2,3},{3,2},{4,5},{5,4},{6,7},{7,6},{8,9},{9,8},{10,11... | collective-permute-start | bytes 1179656 | tf_op jit(solution)/shard_map/token_grads/ppermute | solution.py:668
  276.2 29.7 %collective-permute-start.28 = (bf16[256,768]{1,0:T(8,128)(2,1)}, bf16[256,768]{1,0:T(8,128)(2,1)S(1)}, u32[]{:S(2)}, u32[]{:S(2)}) collective-permute-start(bf16[256,768]{1,0:T(8,128)(2,1)} %get-tuple-element.144), channel_id=1, source_target_pairs={{0,3},{1,2},{2,1},{3,0},{4,7},{5,6},{6,5},{7,4},{8,11},{9,10},{10,... | collective-permute-start | bytes 1179656 | tf_op jit(solution)/shard_map/token_grads/ppermute | solution.py:668
  298.8 15.4 %collective-permute-start.27 = (bf16[256,768]{1,0:T(8,128)(2,1)}, bf16[256,768]{1,0:T(8,128)(2,1)S(1)}, u32[]{:S(2)}, u32[]{:S(2)}) collective-permute-start(bf16[256,768]{1,0:T(8,128)(2,1)} %get-tuple-element.145), channel_id=1, source_target_pairs={{0,2},{1,3},{2,0},{3,1},{4,6},{5,7},{6,4},{7,5},{8,10},{9,11},{10,... | collective-permute-start | bytes 1179656 | tf_op jit(solution)/shard_map/token_grads/ppermute | solution.py:668
  305.9 16.0 %collective-permute-start.35 = (bf16[384,640]{1,0:T(8,128)(2,1)S(1)}, bf16[384,640]{1,0:T(8,128)(2,1)S(1)}, u32[]{:S(2)}, u32[]{:S(2)}) collective-permute-start(bf16[384,640]{1,0:T(8,128)(2,1)S(1)} %get-tuple-element.147), channel_id=1, source_target_pairs={{0,16},{1,17},{2,18},{3,19},{4,20},{5,21},{6,22},{7,23},{8,24},{9,... | collective-permute-start | bytes 1474568 | tf_op jit(solution)/shard_map/group_weight_grads/ppermute | solution.py:668
  318.5 16.8 %collective-permute-start.43 = (bf16[24,3840]{1,0:T(8,128)(2,1)S(1)}, bf16[24,3840]{1,0:T(8,128)(2,1)S(1)}, u32[]{:S(2)}, u32[]{:S(2)}) collective-permute-start(bf16[24,3840]{1,0:T(8,128)(2,1)S(1)} %get-tuple-element.156), channel_id=1, source_target_pairs={{0,12},{1,13},{2,14},{3,15},{4,8},{5,9},{6,10},{7,11},{8,4},{9,5},... | collective-permute-start | bytes 552968 | tf_op jit(solution)/shard_map/token_grads/ppermute | solution.py:668
  319.8 21.6 %collective-permute-start.42 = (bf16[24,3840]{1,0:T(8,128)(2,1)S(1)}, bf16[24,3840]{1,0:T(8,128)(2,1)S(1)}, u32[]{:S(2)}, u32[]{:S(2)}) collective-permute-start(bf16[24,3840]{1,0:T(8,128)(2,1)S(1)} %get-tuple-element.157), channel_id=1, source_target_pairs={{0,8},{1,9},{2,10},{3,11},{4,12},{5,13},{6,14},{7,15},{8,0},{9,1},... | collective-permute-start | bytes 552968 | tf_op jit(solution)/shard_map/token_grads/ppermute | solution.py:668
  322.7 26.2 %collective-permute-start.40 = (bf16[96,640]{1,0:T(8,128)(2,1)S(1)}, bf16[96,640]{1,0:T(8,128)(2,1)S(1)}, u32[]{:S(2)}, u32[]{:S(2)}) collective-permute-start(bf16[96,640]{1,0:T(8,128)(2,1)S(1)} %get-tuple-element.164), channel_id=1, source_target_pairs={{0,12},{1,13},{2,14},{3,15},{4,8},{5,9},{6,10},{7,11},{8,4},{9,5},... | collective-permute-start | bytes 368648 | tf_op jit(solution)/shard_map/token_grads/ppermute | solution.py:668
  324.6 24.3 %collective-permute-start.38 = (bf16[96,640]{1,0:T(8,128)(2,1)S(1)}, bf16[96,640]{1,0:T(8,128)(2,1)S(1)}, u32[]{:S(2)}, u32[]{:S(2)}) collective-permute-start(bf16[96,640]{1,0:T(8,128)(2,1)S(1)} %get-tuple-element.165), channel_id=1, source_target_pairs={{0,4},{1,5},{2,6},{3,7},{4,0},{5,1},{6,2},{7,3},{8,12},{9,13},{10,... | collective-permute-start | bytes 368648 | tf_op jit(solution)/shard_map/token_grads/ppermute | solution.py:668
  325.0 23.9 %collective-permute-start.39 = (bf16[96,640]{1,0:T(8,128)(2,1)S(1)}, bf16[96,640]{1,0:T(8,128)(2,1)S(1)}, u32[]{:S(2)}, u32[]{:S(2)}) collective-permute-start(bf16[96,640]{1,0:T(8,128)(2,1)S(1)} %get-tuple-element.166), channel_id=1, source_target_pairs={{0,8},{1,9},{2,10},{3,11},{4,12},{5,13},{6,14},{7,15},{8,0},{9,1},... | collective-permute-start | bytes 368648 | tf_op jit(solution)/shard_map/token_grads/ppermute | solution.py:668
  344.8 13.0 %collective-permute-start.37 = (bf16[128,768]{1,0:T(8,128)(2,1)S(1)}, bf16[128,768]{1,0:T(8,128)(2,1)S(1)}, u32[]{:S(2)}, u32[]{:S(2)}) collective-permute-start(bf16[128,768]{1,0:T(8,128)(2,1)S(1)} %get-tuple-element.175), channel_id=1, source_target_pairs={{0,4},{1,5},{2,6},{3,7},{4,0},{5,1},{6,2},{7,3},{8,20},{9,21},{10,... | collective-permute-start | bytes 589832 | tf_op jit(solution)/shard_map/token_grads/ppermute | solution.py:668
  (64 other events, 433.7 us)
Sparse Core Ops, SparseCore 0:
  11.5 116.9 all-gather.1
